TPU v7x, 32 devices: a whole 2x2x4 slice. The times are simulated.
32 devices in a mesh: groups: 2 (over y), seq: 4 (over z), chan: 4 (over x, core).
Axes of the slice: x: 2, y: 2, z: 4, core: 2. Of those that a mesh axis runs over, the one named last changes fastest.
Arguments:
- x_in: bfloat16 [3072, 8192], P(('groups', 'seq'), 'chan'), parts along dimension 0, may hold values from -6 to 6
- b_in: bfloat16 [3072, 8, 128], P(('groups', 'seq'), 'chan'), parts along dimension 0, may hold values from -6 to 6
- c_in: bfloat16 [3072, 8, 128], P(('groups', 'seq'), 'chan'), parts along dimension 0, may hold values from -6 to 6
- dt_in: float32 [3072, 128], P(('groups', 'seq'), 'chan'), parts along dimension 0, may hold values from -1.1 to 3.3
- a_log: float32 [128], P('chan'), may hold values from -11 to -3.4
- z_in: bfloat16 [3072, 8192], P(('groups', 'seq'), 'chan'), parts along dimension 0, may hold values from -6 to 6
- conv_x: float32 [4, 8192], P(None, 'chan'), may hold values from -3 to 3
- conv_bc: float32 [2, 4, 8, 128], P(None, None, 'chan'), may hold values from -3 to 3
- norm_gain: float32 [8192], P('chan'), may hold values from 0.25 to 1.75
- w_kv: bfloat16 [8192, 8, 256], P('chan'), may hold values from -1 to 1
- queries: bfloat16 [3072, 64, 128], P(('groups', 'seq'), 'chan'), parts along dimension 0, may hold values from -40 to 40
Outputs:
- mixer_out: bfloat16 [3072, 8192], P(('groups', 'seq'), 'chan'), parts along dimension 0
- attn_out: bfloat16 [3072, 64, 128], P(('groups', 'seq'), 'chan'), parts along dimension 0
There are 2 independent parts, one for each index of `groups`. A program takes and returns all parts, laid end to end along the dimension named above; an argument that names none is the same for every part. Nothing has to cross between parts.
All inputs are finite; a program needn't handle non-finite values.
Results may differ from a plain program's by a relative error of at most 0.0045.
Values may be sent and summed in bfloat16 or wider, within the bound.
A program may use at most 64 MiB of HBM per device.

v0:
```python
import jax
import jax.numpy as jnp
from jax import lax
from jax.sharding import PartitionSpec as P

STRETCH = 128


HIGHEST = lax.Precision.HIGHEST


def shifted(value, axis, steps):
    count = lax.axis_size(axis)
    leading, last = (max(0, -steps), min(count, count - steps))
    return lax.ppermute(value, axis, [(source, source + steps) for source in range(leading, last)])


def silu_of(values):
    return values * jax.nn.sigmoid(values)


def rounded(values):
    return lax.optimization_barrier(values.astype(jnp.bfloat16))


def causal_conv(extended, conv_taps, token_count):
    summed = jnp.zeros((token_count,) + extended.shape[1:], jnp.float32)
    for offset in range(conv_taps.shape[0]):
        summed = summed + conv_taps[offset] * extended[offset : offset + token_count]
    return summed


def stretch_scan(x_heads, b_rows, c_rows, step_rows, decay_rates, initial):
    length = STRETCH
    blocks = x_heads.shape[0] // length
    causal_mask = (jnp.arange(length)[:, None] >= jnp.arange(length)[None, :])[:, :, None, None]

    def advance(carried, pieces):
        x_block, b_block, c_block, step_block = pieces
        running = jnp.cumsum(-step_block * decay_rates, axis=0)
        spread = running[:, None] - running[None, :]
        decays = jnp.where(causal_mask, jnp.exp(jnp.where(causal_mask, spread, 0.0)), 0.0)
        intersection = jnp.einsum("tgn,sgn->tsg", c_block, b_block, precision=HIGHEST)
        mixing = decays * intersection[..., None] * step_block[None]
        within = jnp.einsum("tsgh,sghp->tghp", mixing, x_block, precision=HIGHEST)
        before = (
            jnp.einsum("tgn,ghpn->tghp", c_block, carried, precision=HIGHEST)
            * jnp.exp(running)[..., None]
        )
        tail_weight = jnp.exp(running[-1][None] - running) * step_block
        carried = carried * jnp.exp(running[-1])[..., None, None] + jnp.einsum(
            "sgh,sghp,sgn->ghpn", tail_weight, x_block, b_block, precision=HIGHEST
        )
        return (carried, within + before)

    def to_blocks(values_in):
        return values_in.reshape((blocks, length) + values_in.shape[1:])

    last_state, outputs = lax.scan(
        advance,
        initial,
        (to_blocks(x_heads), to_blocks(b_rows), to_blocks(c_rows), to_blocks(step_rows)),
    )
    return (outputs.reshape(x_heads.shape), last_state)


def on_device(x_in, b_in, c_in, dt_in, a_log, z_in, conv_x, conv_bc, norm_gain, w_kv, queries):
    tokens, channels = x_in.shape
    groups_here = b_in.shape[1]
    state_width = b_in.shape[2]
    heads_here = dt_in.shape[1]
    per_group = heads_here // groups_here
    head_width = channels // heads_here
    margin = conv_x.shape[0] - 1
    flat_width = groups_here * state_width
    seq_index = lax.axis_index("seq")
    seq_count = lax.axis_size("seq")
    rim_source = jnp.concatenate(
        [
            x_in[tokens - margin :],
            b_in[tokens - margin :].reshape(margin, flat_width),
            c_in[tokens - margin :].reshape(margin, flat_width),
        ],
        axis=1,
    )
    rim_rows = shifted(rim_source, "seq", 1)
    x_padded = jnp.concatenate([rim_rows[:, :channels], x_in], axis=0).astype(jnp.float32)
    b_padded = jnp.concatenate(
        [
            rim_rows[:, channels : channels + flat_width].reshape(margin, groups_here, state_width),
            b_in,
        ],
        axis=0,
    ).astype(jnp.float32)
    c_padded = jnp.concatenate(
        [rim_rows[:, channels + flat_width :].reshape(margin, groups_here, state_width), c_in],
        axis=0,
    ).astype(jnp.float32)
    x_conv = rounded(silu_of(causal_conv(x_padded, conv_x, tokens)))
    b_rows = rounded(silu_of(causal_conv(b_padded, conv_bc[0], tokens))).astype(jnp.float32)
    c_rows = rounded(silu_of(causal_conv(c_padded, conv_bc[1], tokens))).astype(jnp.float32)
    step_sizes = jax.nn.softplus(dt_in).reshape(tokens, groups_here, per_group)
    decay_rates = jnp.exp(a_log).reshape(groups_here, per_group)
    x_heads = x_conv.astype(jnp.float32).reshape(tokens, groups_here, per_group, head_width)
    zero_state = jnp.zeros((groups_here, per_group, head_width, state_width), jnp.float32)
    local_out, local_state = stretch_scan(
        x_heads, b_rows, c_rows, step_sizes, decay_rates, zero_state
    )
    running = jnp.cumsum(-step_sizes * decay_rates, axis=0)
    totals = running[-1]
    all_totals = lax.all_gather(totals[None], "seq", axis=0, tiled=True)
    device_rank = jnp.arange(all_totals.shape[0])
    between = (device_rank[None, :] > device_rank[:, None]) & (device_rank[None, :] < seq_index)
    exponent = jnp.einsum("jk,kgh->jgh", between.astype(jnp.float32), all_totals, precision=HIGHEST)
    weights_all = jnp.where((device_rank < seq_index)[:, None, None], jnp.exp(exponent), 0.0)
    incoming = zero_state + jnp.einsum(
        "jgh,jghpn->ghpn",
        weights_all,
        lax.all_gather(local_state[None].astype(jnp.bfloat16), "seq", axis=0, tiled=True).astype(
            jnp.float32
        ),
        precision=HIGHEST,
    )
    carried_in = (
        jnp.einsum("tgn,ghpn->tghp", c_rows, incoming, precision=HIGHEST)
        * jnp.exp(running)[..., None]
    )
    ssm_out = (local_out + carried_in).reshape(tokens, channels)
    gated_out = ssm_out * silu_of(z_in.astype(jnp.float32))
    grouped = gated_out.reshape(tokens, groups_here, channels // groups_here)
    normed = grouped * lax.rsqrt(jnp.mean(grouped * grouped, axis=-1, keepdims=True) + 1e-05)
    mixer_out = (normed.reshape(tokens, channels) * norm_gain).astype(jnp.bfloat16)
    kv_here = w_kv.shape[1] // lax.axis_size("chan")
    kv_mine = lax.psum_scatter(
        jnp.einsum("tc,chk->htk", mixer_out, w_kv, preferred_element_type=jnp.float32),
        "chan",
        scatter_dimension=0,
        tiled=True,
    )
    att_width = queries.shape[2]
    keys_raw = kv_mine[..., :att_width]
    key_hat = (
        keys_raw * lax.rsqrt(jnp.mean(keys_raw * keys_raw, axis=-1, keepdims=True) + 1e-06)
    ).astype(jnp.bfloat16)
    keyval = jnp.concatenate([key_hat, kv_mine[..., att_width:].astype(jnp.bfloat16)], axis=-1)
    query_f = queries.astype(jnp.float32)
    query_hat = (
        query_f * lax.rsqrt(jnp.mean(query_f * query_f, axis=-1, keepdims=True) + 1e-06)
    ).astype(jnp.bfloat16)
    positions = seq_index * tokens + jnp.arange(tokens)
    query_rows = query_hat.shape[0]
    group_size = queries.shape[1] // kv_here
    active_heads = query_hat.reshape(query_rows, kv_here, group_size, att_width)
    top_position = jnp.max(positions)
    score_scale = att_width ** (-0.5)
    zero_numerator = jnp.zeros((query_rows, kv_here, group_size, att_width), jnp.float32)
    zero_denominator = jnp.zeros((query_rows, kv_here, group_size), jnp.float32)

    def attend_piece(carried, shard_rows, first_row):
        numerator, denominator = carried
        span = shard_rows.shape[1]
        keys_here = shard_rows[..., :att_width]
        values_here = shard_rows[..., att_width:]
        scores = (
            jnp.einsum(
                "tkga,kja->tkgj", active_heads, keys_here, preferred_element_type=jnp.float32
            )
            * score_scale
        )
        key_positions = first_row + jnp.arange(span)
        allowed = (positions[:, None] >= key_positions[None, :])[:, None, None, :]
        weights = jnp.where(allowed, jnp.exp(scores), 0.0)
        numerator = numerator + jnp.einsum(
            "tkgj,kja->tkga",
            weights.astype(jnp.bfloat16),
            values_here,
            preferred_element_type=jnp.float32,
        )
        denominator = denominator + jnp.sum(weights, axis=-1)
        return (numerator, denominator)

    block_shards = 1
    while block_shards * 2 <= seq_count and block_shards * 2 * tokens <= 1024:
        block_shards = block_shards * 2
    block_width = block_shards * tokens
    everything = lax.all_gather(keyval, "seq", axis=1, tiled=True)
    needed = top_position // block_width + 1

    def step_block(block_index, carried):
        first_row = block_index * block_width
        shard_rows = lax.dynamic_slice_in_dim(everything, first_row, block_width, 1)
        return attend_piece(carried, shard_rows, first_row)

    numerator, denominator = lax.fori_loop(
        0, needed, step_block, (zero_numerator, zero_denominator)
    )
    attn_out = (
        (numerator / denominator[..., None])
        .astype(jnp.bfloat16)
        .reshape(query_rows, kv_here * group_size, att_width)
    )
    return (mixer_out, attn_out)


def solution(mesh):
    return jax.shard_map(
        on_device,
        mesh=mesh,
        in_specs=(
            P(("groups", "seq"), "chan"),
            P(("groups", "seq"), "chan", None),
            P(("groups", "seq"), "chan", None),
            P(("groups", "seq"), "chan"),
            P("chan"),
            P(("groups", "seq"), "chan"),
            P(None, "chan"),
            P(None, None, "chan", None),
            P("chan"),
            P("chan", None, None),
            P(("groups", "seq"), "chan", None),
        ),
        out_specs=(P(("groups", "seq"), "chan"), P(("groups", "seq"), "chan", None)),
        check_vma=False,
    )
```

profile of v0, /device:TPU:24, one launch (start us, length us, event | category | flops | bytes accessed | tf_op | source)
XLA Modules:
  0.0 340.7 jit_solution(13398811264598712426)
XLA Ops:
  21.3 5.7 %reshape.194 = f32[3,128,2,16,64]{4,3,2,1,0:T(8,128)} reshape(bf16[384,2048]{1,0:T(8,128)(2,1)} %multiply_convert_fusion.1) | data formatting | bytes 4718592 | tf_op jit(solution)/shard_map/reshape;reshape | solution.py:57
  27.0 6.8 %copy.111 = f32[3,128,2,16,64]{1,4,3,2,0:T(8,128)} copy(f32[3,128,2,16,64]{4,3,2,1,0:T(8,128)} %reshape.194) | data formatting | bytes 6291456
  33.8 110.8 %while.28 = (s32[]{:T(128)}, f32[2,16,64,128]{3,2,1,0:T(8,128)S(1)}, f32[3,128,2,16,64]{1,0,4,3,2:T(4,128)}, f32[3,128,2,16]{1,0,3,2:T(4,128)S(1)}, f32[32]{0:T(...) while((s32[]{:T(128)}, ...), condition=%wide.region_2.3_spmd.clone.clone, body=%wide.region_0.2_spmd.clone.clone.sunk | while | flops 1263300608 | bytes 11948679 | solution.py:59
  35.2 5.5 %fusion.138 = f32[128,2,16,64]{0,3,2,1:T(8,128)S(1)} fusion(f32[128,2,16]{0,2,1:T(8,128)S(1)} %copy.178, f32[128,128,2]{1,0,2:T(8,128)S(1)} %copy.179, f32[128,2,16]{0,2,1:T(8,128)S(1)} %copy.180, pred[128,128]{1,0:T(8,128)(4,1)S(1)} %fusion.137, f32[3,128,2,16,64]{1,4,3,2,0:T(8,128)} %get-tuple-element.383, s32[]{:T(128)S(6)} %copy.186), kind=kOutput, calls=%fused_computation.27.clone.1 | convolution fusion | flops 405274624 | bytes 2293764 | tf_op jit(solution)/shard_map/while/body/eval_jaxpr/tsgh,sghp->tghp/dot_general | solution.py:45
  44.3 26.4 %dynamic_update_slice.7 = f32[3,128,2,16,64]{1,0,4,3,2:T(4,128)} dynamic-update-slice(f32[3,128,2,16,64]{1,0,4,3,2:T(4,128)} %get-tuple-element.370, f32[1,128,2,16,64]{1,0,4,3,2:T(1,128)S(1)} %bitcast.207, s32[]{:T(128)S(6)} %copy.186, s32[]{:T(128)} %constant.39.clone.1..sunk.1, s32[]{:T(128)} %constant.39.clone.1..sunk.1, s32[]{:T(128)} %constant.39.clone.1..sunk.1, s32[]{:T(128)} %constant.39.clone.1..sunk.1) | dynamic-update-slice | bytes 2097156 | tf_op jit(solution)/shard_map/while/body/jit(dynamic_update_index_in_dim)/dynamic_update_slice | solution.py:59
  72.1 5.5 %fusion.138 = f32[128,2,16,64]{0,3,2,1:T(8,128)S(1)} fusion(f32[128,2,16]{0,2,1:T(8,128)S(1)} %copy.178, f32[128,128,2]{1,0,2:T(8,128)S(1)} %copy.179, f32[128,2,16]{0,2,1:T(8,128)S(1)} %copy.180, pred[128,128]{1,0:T(8,128)(4,1)S(1)} %fusion.137, f32[3,128,2,16,64]{1,4,3,2,0:T(8,128)} %get-tuple-element.383, s32[]{:T(128)S(6)} %copy.186), kind=kOutput, calls=%fused_computation.27.clone.1 | convolution fusion | flops 405274624 | bytes 2293764 | tf_op jit(solution)/shard_map/while/body/eval_jaxpr/tsgh,sghp->tghp/dot_general | solution.py:45
  81.2 26.4 %dynamic_update_slice.7 = f32[3,128,2,16,64]{1,0,4,3,2:T(4,128)} dynamic-update-slice(f32[3,128,2,16,64]{1,0,4,3,2:T(4,128)} %get-tuple-element.370, f32[1,128,2,16,64]{1,0,4,3,2:T(1,128)S(1)} %bitcast.207, s32[]{:T(128)S(6)} %copy.186, s32[]{:T(128)} %constant.39.clone.1..sunk.1, s32[]{:T(128)} %constant.39.clone.1..sunk.1, s32[]{:T(128)} %constant.39.clone.1..sunk.1, s32[]{:T(128)} %constant.39.clone.1..sunk.1) | dynamic-update-slice | bytes 2097156 | tf_op jit(solution)/shard_map/while/body/jit(dynamic_update_index_in_dim)/dynamic_update_slice | solution.py:59
  109.0 5.5 %fusion.138 = f32[128,2,16,64]{0,3,2,1:T(8,128)S(1)} fusion(f32[128,2,16]{0,2,1:T(8,128)S(1)} %copy.178, f32[128,128,2]{1,0,2:T(8,128)S(1)} %copy.179, f32[128,2,16]{0,2,1:T(8,128)S(1)} %copy.180, pred[128,128]{1,0:T(8,128)(4,1)S(1)} %fusion.137, f32[3,128,2,16,64]{1,4,3,2,0:T(8,128)} %get-tuple-element.383, s32[]{:T(128)S(6)} %copy.186), kind=kOutput, calls=%fused_computation.27.clone.1 | convolution fusion | flops 405274624 | bytes 2293764 | tf_op jit(solution)/shard_map/while/body/eval_jaxpr/tsgh,sghp->tghp/dot_general | solution.py:45
  118.2 26.4 %dynamic_update_slice.7 = f32[3,128,2,16,64]{1,0,4,3,2:T(4,128)} dynamic-update-slice(f32[3,128,2,16,64]{1,0,4,3,2:T(4,128)} %get-tuple-element.370, f32[1,128,2,16,64]{1,0,4,3,2:T(1,128)S(1)} %bitcast.207, s32[]{:T(128)S(6)} %copy.186, s32[]{:T(128)} %constant.39.clone.1..sunk.1, s32[]{:T(128)} %constant.39.clone.1..sunk.1, s32[]{:T(128)} %constant.39.clone.1..sunk.1, s32[]{:T(128)} %constant.39.clone.1..sunk.1) | dynamic-update-slice | bytes 2097156 | tf_op jit(solution)/shard_map/while/body/jit(dynamic_update_index_in_dim)/dynamic_update_slice | solution.py:59
  147.9 8.6 %all_gather.9 = f32[4,2,16]{2,1,0:T(2,128)S(1)} all-gather(f32[1,2,16]{2,1,0:T(2,128)S(1)} %copy.117), channel_id=1, replica_groups=mesh['groups'=2,'seq'=4,'chan'=4] {'seq'}, dimensions={0}, use_global_device_ids=true | all-gather | bytes 640 | tf_op jit(solution)/shard_map/all_gather | solution.py:111
  156.8 4.6 %reshape.173 = f32[384,2,16,64]{0,3,2,1:T(8,128)S(1)} reshape(f32[3,128,2,16,64]{1,0,4,3,2:T(4,128)} %get-tuple-element.92) | data formatting | bytes 6291456 | tf_op jit(solution)/shard_map/reshape | solution.py:64
  161.4 30.2 %all-gather.6.cloned.1.call-done = bf16[8,16,64,128]{3,2,1,0:T(8,128)(2,1)} async-done(((bf16[2,16,64,128]{3,2,1,0:T(8,128)(2,1)}), bf16[8,16,64,128]{3,2,1,0:T(8,128)(2,1)}) %all-gather.6.cloned.1.call-update) | async-done | bytes 2097168 | tf_op jit(solution)/shard_map/all_gather | solution.py:119
  191.6 5.5 %fusion.76 = f32[2,16,1,64,128]{4,2,3,1,0:T(1,128)S(1)} fusion(f32[4,2,16,1,1]{0,3,4,2,1:T(1,128)S(1)} %copy.132, bf16[4,2,16,64,128]{4,3,2,1,0:T(8,128)(2,1)} %bitcast.224), kind=kOutput, calls=%fused_computation.96 | convolution fusion | flops 12582912 | bytes 3146240 | tf_op jit(solution)/shard_map/jgh,jghpn->ghpn/dot_general | solution.py:116
  197.1 3.2 fusion.75
  202.7 3.9 %fusion.98 = f32[384,2048]{1,0:T(8,128)} fusion(f32[384,2048]{1,0:T(8,128)S(1)} %copy.119, bf16[384,2048]{1,0:T(8,128)(2,1)} %param.20), kind=kLoop, calls=%fused_computation.160 | loop fusion | flops 5505024 | bytes 7864320 | tf_op jit(solution)/shard_map/mul | solution.py:131
  206.6 5.6 %mul.302 = f32[384,2,1024]{2,1,0:T(2,128)} reshape(f32[384,2048]{1,0:T(8,128)} %fusion.98) | data formatting | bytes 6291456 | tf_op jit(solution)/shard_map/mul | solution.py:131
  220.1 5.1 %fusion.78 = f32[8,384,256]{2,1,0:T(8,128)} fusion(bf16[2048,8,256]{2,1,0:T(8,128)(2,1)S(1)} %bitcast.223, bf16[384,2048]{1,0:T(8,128)(2,1)S(1)} %multiply_convert_fusion), kind=kOutput, calls=%fused_computation.98 | convolution fusion | flops 3221225472 | bytes 13107200 | tf_op jit(solution)/shard_map/tc,chk->htk/dot_general | solution.py:135
  225.3 39.0 %reduce-scatter.2.cloned.1.call-done = f32[2,384,256]{2,1,0:T(8,128)} async-done(((f32[8,384,256]{2,1,0:T(8,128)}), f32[2,384,256]{2,1,0:T(8,128)}) %reduce-scatter.2.cloned.1.call-update) | async-done | bytes 786448 | tf_op jit(solution)/shard_map/reduce_scatter | solution.py:134
  274.7 28.9 %all-gather.4.cloned.1.call-done = bf16[2,1536,256]{2,1,0:T(8,128)(2,1)} async-done(((bf16[2,384,256]{2,1,0:T(8,128)(2,1)}), bf16[2,1536,256]{2,1,0:T(8,128)(2,1)}) %all-gather.4.cloned.1.call-update) | async-done | bytes 1572880 | tf_op jit(solution)/shard_map/all_gather | solution.py:186
  305.6 24.4 %while.27 = (s32[]{:T(128)}, f32[384,2,8,128]{0,3,2,1:T(8,128)}, f32[384,2,8]{0,2,1:T(8,128)S(1)}, s32[]{:T(128)}, bf16[2,1536,256]{2,1,0:T(8,128)(2,1)}, /*inde...) while((s32[]{:T(128)}, f32[384,2,8,128]{0,3,2,1:T(8,128)}, ...), condition=%wide.region_12.13_spmd.clone, body=%wide.region_10.12_spmd.clone.sunk | while | flops 2445313024 | bytes 47391936 | solution.py:194
  305.9 5.5 %fusion.125 = (f32[384,2,8]{0,2,1:T(8,128)S(1)}, f32[2,768,384,8]{2,1,3,0:T(8,128)S(1)}) fusion(pred[384,768]{0,1:T(8,128)(4,1)S(1)} %broadcast_compare_fusion.2, bf16[384,2,8,128]{3,0,2,1:T(8,128)(2,1)} %get-tuple-element.417, bf16[2,1536,256]{2,1,0:T(8,128)(2,1)} %get-tuple-element.416, s32[]{:T(128)S(6)} %select_n.69), kind=kOutput, calls=%fused_computation.3.clone.1 | convolution fusion | flops 1222109184 | bytes 21159940 | tf_op jit(solution)/shard_map/while/body/tkga,kja->tkgj/dot_general | solution.py:165
  311.4 6.4 %bitcast_add_fusion.2 = f32[384,2,8,128]{0,3,2,1:T(8,128)} fusion(f32[384,2,8,128]{0,3,2,1:T(8,128)} %get-tuple-element.401, f32[2,768,384,8]{2,1,3,0:T(8,128)S(1)} %get-tuple-element.346, pred[384,768]{0,1:T(8,128)(4,1)S(1)} %broadcast_compare_fusion.2, bf16[2,1536,256]{2,1,0:T(8,128)(2,1)} %get-tuple-element.416, s32[]{:T(128)S(6)} %select_n.69, ...), kind=kOutput, calls=%fused_computation.9.clone.1 | convolution fusion | flops 1222901760 | bytes 25853960 | tf_op jit(solution)/shard_map/while/body/tkgj,kja->tkga/dot_general | solution.py:173
  318.1 5.5 %fusion.125 = (f32[384,2,8]{0,2,1:T(8,128)S(1)}, f32[2,768,384,8]{2,1,3,0:T(8,128)S(1)}) fusion(pred[384,768]{0,1:T(8,128)(4,1)S(1)} %broadcast_compare_fusion.2, bf16[384,2,8,128]{3,0,2,1:T(8,128)(2,1)} %get-tuple-element.417, bf16[2,1536,256]{2,1,0:T(8,128)(2,1)} %get-tuple-element.416, s32[]{:T(128)S(6)} %select_n.69), kind=kOutput, calls=%fused_computation.3.clone.1 | convolution fusion | flops 1222109184 | bytes 21159940 | tf_op jit(solution)/shard_map/while/body/tkga,kja->tkgj/dot_general | solution.py:165
  323.6 6.4 %bitcast_add_fusion.2 = f32[384,2,8,128]{0,3,2,1:T(8,128)} fusion(f32[384,2,8,128]{0,3,2,1:T(8,128)} %get-tuple-element.401, f32[2,768,384,8]{2,1,3,0:T(8,128)S(1)} %get-tuple-element.346, pred[384,768]{0,1:T(8,128)(4,1)S(1)} %broadcast_compare_fusion.2, bf16[2,1536,256]{2,1,0:T(8,128)(2,1)} %get-tuple-element.416, s32[]{:T(128)S(6)} %select_n.69, ...), kind=kOutput, calls=%fused_computation.9.clone.1 | convolution fusion | flops 1222901760 | bytes 25853960 | tf_op jit(solution)/shard_map/while/body/tkgj,kja->tkga/dot_general | solution.py:173
  (137 shorter events, 57.6 us)
Async XLA Ops:
  7.2 184.4 %all-gather.6.cloned.1.call-start = ((), (), s32[]{:S(2)}) async-start(), calls=%async_computation.3 | async-start | bytes 2621440 | tf_op jit(solution)/shard_map/all_gather | solution.py:119
  9.4 6.5 %collective-permute-start = (bf16[3,2560]{1,0:T(4,128)(2,1)S(1)}, bf16[3,2560]{1,0:T(4,128)(2,1)S(1)}, u32[]{:S(2)}, u32[]{:S(2)}) collective-permute-start(bf16[3,2560]{1,0:T(4,128)(2,1)S(1)} %pad_maximum_fusion.1), channel_id=1, source_target_pairs={{0,4},{4,8},{8,12},{1,5},{5,9},{9,13},{2,6},{6,10},{10,14},{3,7},{... | collective-permute-start | bytes 46088 | tf_op jit(solution)/shard_map/ppermute | solution.py:15
  145.5 118.7 %reduce-scatter.2.cloned.1.call-start = ((), (), s32[]{:S(2)}) async-start(), calls=%async_computation.1 | async-start | bytes 3932160 | tf_op jit(solution)/shard_map/reduce_scatter | solution.py:134
  215.1 5.0 %slice-start = ((s8[8388608]{0:T(1024)(128)(4,1)}), s8[4194304]{0:T(1024)(128)(4,1)S(1)}, s32[]{:S(2)}) async-start(s8[8388608]{0:T(1024)(128)(4,1)} %bitcast.222), calls=%async_computation.4 | async-start | bytes 8388608
  216.0 1.8 copy-start.1
  216.0 1.8 copy-start.3
  216.0 4.1 %slice-start.1 = ((s8[8388608]{0:T(1024)(128)(4,1)}), s8[4194304]{0:T(1024)(128)(4,1)S(1)}, s32[]{:S(2)}) async-start(s8[8388608]{0:T(1024)(128)(4,1)} %bitcast.222), calls=%async_computation.5 | async-start | bytes 8388608
  218.9 1.1 copy-start.2
  225.2 45.8 %copy-start = (bf16[384,16,128]{2,1,0:T(8,128)(2,1)S(1)}, bf16[384,16,128]{2,1,0:T(8,128)(2,1)}, u32[]{:S(2)}) copy-start(bf16[384,16,128]{2,1,0:T(8,128)(2,1)} %param.25) | copy-start | bytes 4718596
  225.2 78.4 %all-gather.4.cloned.1.call-start = ((), (), s32[]{:S(2)}) async-start(), calls=%async_computation.2 | async-start | bytes 1966080 | tf_op jit(solution)/shard_map/all_gather | solution.py:186
Sparse Core Ops, SparseCore 0:
  145.7 45.9 all-gather.5
  225.3 38.8 reduce-scatter.1
  268.6 35.0 all-gather.3
where the time goes:
time: 345 us; the launch traced here: 341 us
  local copies, waits for them, and re-layouts  124 us (36%)
  waiting for transfers between devices  98.2 us (28%)
  matrix products  66.3 us (19%)
  other arithmetic  26.3 us (8%)
  between operations  16 us (5%)
  blocking collectives  8.58 us (2%)
    dynamic_update_slice x3, local copies, waits for them, and re-layouts, stretch_scan(): lax.scan(advance, initial, (to_blocks(x_heads), to_blocks(b_rows), to_blo...  79.3 us
    reduce_scatter x1, waiting for transfers between devices, on_device(): lax.psum_scatter(jnp.einsum('tc,chk->htk', mixer_out, w_kv, preferred_ele...  39 us
    all_gather x1, waiting for transfers between devices, on_device(): lax.all_gather(local_state[None].astype(jnp.bfloat16), 'seq', axis=0, til...  30.2 us
    all_gather x1, waiting for transfers between devices, on_device(): everything = lax.all_gather(keyval, 'seq', axis=1, tiled=True)  28.9 us
    dot_general x3, matrix products, advance(): within = jnp.einsum('tsgh,sghp->tghp', mixing, x_block, precision=HIGHEST)  16.6 us
    unnamed x18, local copies, waits for them, and re-layouts  12.9 us
    dot_general x2, matrix products, attend_piece(): jnp.einsum('tkgj,kja->tkga', weights.astype(jnp.bfloat16), values_here, p...  12.9 us
    dot_general x2, matrix products, attend_piece(): jnp.einsum('tkga,kja->tkgj', active_heads, keys_here, preferred_element_t...  11 us
  transfers between devices with their start and end apart: 4, of which 3 were waited for; matrix products, arithmetic and copies ran while one was open for 5% of the time, Pallas kernels for 0%

commit v1 on v0

v1 whole, which is shorter than its diff:
```python
import functools
import math

import jax
import jax.numpy as jnp
from jax import lax
from jax.experimental import pallas as pl
from jax.experimental.pallas import tpu as pltpu
from jax.sharding import PartitionSpec as P

MESH = pl.DeviceIdType.MESH
F32 = jnp.float32
BF16 = jnp.bfloat16
RIM = 16
CORES = 2
WIDE = 256
ROWS = 512


def mm(a, b):
    return jnp.dot(a, b, preferred_element_type=F32)


def contract_rows(a, b):
    return lax.dot_general(a, b, (((0,), (0,)), ((), ())), preferred_element_type=F32)


def contract_lanes(a, b):
    return lax.dot_general(a, b, (((1,), (1,)), ((), ())), preferred_element_type=F32)


def silu(v):
    return v / (1.0 + jnp.exp(-v))


def split2(v):
    high = v.astype(BF16)
    return high, (v - high.astype(F32)).astype(BF16)


def kernel(
    nseq, nchan, nstate, kv_heads,
    x_ref, bc_ref, dt_ref, alog_ref, tx_ref, tbc_ref, gain_ref, z_hbm, w_hbm, q_hbm,
    mix_ref, att_ref,
    zv, wv, qv, rimx, rimbc, xp, bcp, bcv, mask_cb, decay, xs, sl, sin, sout, ybuf, ssq,
    wp, kvp, s1, r1, s2, r2, kvall, qh, acc,
    in_sem, rim_send, rim_recv, st_send, st_recv,
    c1_send, c1_recv, c2_send, c2_recv, kv_send, kv_recv,
):
    tokens, channels = x_ref.shape
    heads = dt_ref.shape[1]
    head_width = channels // heads
    gn = bc_ref.shape[1] // 2
    ngroups = gn // nstate
    nch, _, cw = xs.shape
    per = nch // ngroups
    chg = channels // ngroups
    kvh = kv_heads // nchan
    att = qv.shape[2]
    gs = qv.shape[1] // kvh
    margin = tx_ref.shape[0] - 1
    base = 8 - margin
    nx = nchan // CORES
    me = lax.axis_index("seq")
    chan = lax.axis_index("chan")
    mx = chan // CORES
    core = chan % CORES
    mate = 1 - core
    mate_id = mx * CORES + mate

    def remote(src, dst, ss, rs, where):
        return pltpu.make_async_remote_copy(
            src_ref=src, dst_ref=dst, send_sem=ss, recv_sem=rs, device_id=where, device_id_type=MESH
        )

    z_copy = pltpu.make_async_copy(z_hbm, zv, in_sem.at[0])
    q_copy = pltpu.make_async_copy(q_hbm, qv, in_sem.at[1])
    w_copy = pltpu.make_async_copy(w_hbm, wv, in_sem.at[2])
    z_copy.start()
    q_copy.start()
    w_copy.start()

    barrier = pltpu.get_barrier_semaphore()

    @pl.when(me > 0)
    def _():
        pl.semaphore_signal(barrier, inc=1, device_id={"seq": me - 1}, device_id_type=MESH)

    @pl.when(me < nseq - 1)
    def _():
        pl.semaphore_signal(barrier, inc=1, device_id={"seq": me + 1}, device_id_type=MESH)

    pl.semaphore_signal(barrier, inc=1, device_id={"chan": mate_id}, device_id_type=MESH)
    for off in range(1, nx):
        other = ((mx + off) % nx) * CORES + core
        pl.semaphore_signal(barrier, inc=1, device_id={"chan": other}, device_id_type=MESH)
    pl.semaphore_wait(barrier, nx + jnp.minimum(me, 1) + jnp.minimum(nseq - 1 - me, 1))

    nxt = {"seq": jnp.minimum(me + 1, nseq - 1)}

    def rim_copies():
        return (
            remote(x_ref.at[pl.ds(tokens - RIM, RIM)], rimx, rim_send.at[0], rim_recv.at[0], nxt),
            remote(bc_ref.at[pl.ds(tokens - RIM, RIM)], rimbc, rim_send.at[1], rim_recv.at[1], nxt),
        )

    def state_copy(j):
        return remote(sout.at[j], sin.at[j], st_send.at[j], st_recv.at[j], nxt)

    def kv_copy(src, i):
        return remote(kvall.at[src, i], kvall.at[src, i], kv_send.at[src, i], kv_recv.at[src, i], nxt)

    @pl.when(me < nseq - 1)
    def _():
        for copy in rim_copies():
            copy.start()

    @pl.when(me == 0)
    def _():
        rimx[...] = jnp.zeros_like(rimx)
        rimbc[...] = jnp.zeros_like(rimbc)
        sin[...] = jnp.zeros_like(sin)

    step = jnp.log(1.0 + jnp.exp(dt_ref[...]))
    drop = -step * jnp.exp(alog_ref[...])
    at_row = lax.broadcasted_iota(jnp.int32, (tokens, tokens), 0)
    at_col = lax.broadcasted_iota(jnp.int32, (tokens, tokens), 1)
    causal = at_row >= at_col
    lower = causal.astype(F32).astype(BF16)
    d1, rest = split2(drop)
    d2 = rest
    d3 = (drop - d1.astype(F32) - d2.astype(F32)).astype(BF16)
    running = mm(lower, d1) + mm(lower, d2) + mm(lower, d3)
    e_hi, e_lo = split2(jnp.exp(running))
    w_hi, w_lo = split2(jnp.exp(-running) * step)
    decay[0] = e_hi
    decay[1] = e_lo
    decay[2] = w_hi
    decay[3] = w_lo

    def spread(j):
        head = lax.broadcasted_iota(jnp.int32, (heads, cw), 0) * head_width
        lane = lax.broadcasted_iota(jnp.int32, (heads, cw), 1) + j * cw
        return ((lane >= head) & (lane < head + head_width)).astype(F32).astype(BF16)

    @pl.when(me > 0)
    def _():
        for copy in rim_copies():
            copy.wait_recv()

    bcp[0:8, :] = rimbc[...].astype(F32)[8:16]
    bcp[8 : 8 + tokens, :] = bc_ref[...].astype(F32)
    summed = tbc_ref[0:1, :] * bcp[base : base + tokens, :]
    for k in range(1, margin + 1):
        summed = summed + tbc_ref[k : k + 1, :] * bcp[base + k : base + k + tokens, :]
    bcv[...] = silu(summed).astype(BF16)
    for g in range(ngroups):
        cb = contract_lanes(
            bcv[:, gn + g * nstate : gn + (g + 1) * nstate], bcv[:, g * nstate : (g + 1) * nstate]
        )
        mask_cb[g] = jnp.where(causal, cb, 0.0).astype(BF16)

    def conv_chunk(j, c):
        lanes = pl.ds(pl.multiple_of(j * cw, cw), cw)
        g = j // per
        xp[0:8, :] = rimx[:, lanes].astype(F32)[8:16]
        xp[8 : 8 + tokens, :] = x_ref[:, lanes].astype(F32)
        total = tx_ref[0:1, lanes] * xp[base : base + tokens, :]
        for k in range(1, margin + 1):
            total = total + tx_ref[k : k + 1, lanes] * xp[base + k : base + k + tokens, :]
        conv = silu(total).astype(BF16).astype(F32)
        each = spread(j)
        scaled = (conv * (mm(decay[2], each) + mm(decay[3], each))).astype(BF16)
        xs[j] = scaled
        own = contract_rows(bcv[:, pl.ds(pl.multiple_of(g * nstate, nstate), nstate)], scaled)
        sl[j] = own

        @pl.when(me == 0)
        def _():
            sout[j] = (own * last_decay(j)).astype(BF16)
            state_copy(j).start()

        return c

    def last_decay(j):
        each = spread(j)
        tail = pl.ds(tokens - RIM, RIM)
        return (mm(decay[0, tail, :], each) + mm(decay[1, tail, :], each))[RIM - 1 : RIM, :]

    lax.fori_loop(0, nch, conv_chunk, 0)

    z_copy.wait()
    q_copy.wait()
    w_copy.wait()

    blk = WIDE // kv_heads
    prow = lax.broadcasted_iota(jnp.int32, (WIDE, WIDE), 0)
    pcol = lax.broadcasted_iota(jnp.int32, (WIDE, WIDE), 1)
    perm = (pcol == (prow % blk) * kv_heads + prow // blk).astype(F32).astype(BF16)
    w_parts = channels // blk // nch
    q_rows = tokens // nch

    def filler(j):
        def one(n, c):
            at = j * w_parts + n
            moved = mm(perm, wv[pl.ds(pl.multiple_of(at * WIDE, WIDE), WIDE), :]).astype(BF16)
            for h in range(kv_heads):
                wp[h, pl.ds(pl.multiple_of(at * blk, blk), blk), :] = moved[h * blk : (h + 1) * blk]
            return c

        lax.fori_loop(0, w_parts, one, 0)
        qf = qv[pl.ds(j * q_rows, q_rows)].astype(F32)
        qn = qf * lax.rsqrt(jnp.mean(qf * qf, axis=-1, keepdims=True) + 1e-06)
        for i in range(kvh):
            qh[i, pl.ds(pl.multiple_of(j * q_rows * gs, q_rows * gs), q_rows * gs), :] = (
                qn[:, i * gs : (i + 1) * gs, :].reshape(q_rows * gs, att).astype(BF16)
            )

    def scan_chunk(j, c):
        lanes = pl.ds(pl.multiple_of(j * cw, cw), cw)
        g = j // per

        @pl.when(me > 0)
        def _():
            state_copy(j).wait_recv()

        @pl.when((me > 0) & (me < nseq - 1))
        def _():
            sout[j] = ((sin[j].astype(F32) + sl[j]) * last_decay(j)).astype(BF16)
            state_copy(j).start()

        filler(j)
        each = spread(j)
        gate = silu(zv[:, lanes].astype(F32)) * (mm(decay[0], each) + mm(decay[1], each))
        c_rows = bcv[:, pl.ds(pl.multiple_of(gn + g * nstate, nstate), nstate)]
        y = (mm(mask_cb[g], xs[j]) + mm(c_rows, sin[j])) * gate
        ybuf[j] = y
        sq = y * y
        part = sq[:, 0:128]
        for k in range(1, cw // 128):
            part = part + sq[:, k * 128 : (k + 1) * 128]
        ssq[...] = part + jnp.where(j % per == 0, 0.0, ssq[...])
        return c

    def kv_dot(g, h):
        span = pl.ds(g * chg, chg)
        got = mm(mix_ref[:, span], wp[h, span, :])
        return got if g == 0 else kvp[h] + got

    ssq[...] = jnp.zeros_like(ssq)
    for g in range(ngroups):
        lax.fori_loop(g * per, (g + 1) * per, scan_chunk, 0)
        scale = lax.rsqrt(jnp.sum(ssq[...], axis=-1, keepdims=True) / chg + 1e-05)

        def norm_chunk(j, c):
            lanes = pl.ds(pl.multiple_of(j * cw, cw), cw)
            mix_ref[:, lanes] = (ybuf[j] * scale * gain_ref[0:1, lanes]).astype(BF16)
            return c

        lax.fori_loop(g * per, (g + 1) * per, norm_chunk, 0)
        if g < ngroups - 1:

            def kv_part(h, c):
                kvp[h] = kv_dot(g, h)
                return c

            lax.fori_loop(0, kv_heads, kv_part, 0)

    last = ngroups - 1

    def core_copy(i, cx):
        return remote(
            s1.at[i, cx], r1.at[i, cx], c1_send.at[i, cx], c1_recv.at[i, cx], {"chan": mate_id}
        )

    def chip_copy(i, to, slot):
        return remote(
            s2.at[i, to], r2.at[i, slot], c2_send.at[i, to], c2_recv.at[i, slot],
            {"chan": to * CORES + core},
        )

    for i in range(kvh):

        def to_mate(n, c, i=i):
            cx = (mx + 1 + n) % nx
            s1[i, cx] = kv_dot(last, (cx * CORES + mate) * kvh + i).astype(BF16)
            core_copy(i, cx).start()
            return c

        lax.fori_loop(0, nx, to_mate, 0)
    for i in range(kvh):

        def to_chip(n, c, i=i):
            cx = (mx + 1 + n) % nx
            h = (cx * CORES + core) * kvh + i
            mine = kv_dot(last, h)
            core_copy(i, cx).wait_recv()
            both = mine + r1[i, cx].astype(F32)
            kvp[h] = both

            @pl.when(n < nx - 1)
            def _():
                s2[i, cx] = both.astype(BF16)
                chip_copy(i, cx, mx).start()

            return c

        lax.fori_loop(0, nx, to_chip, 0)

    factor = att ** (-0.5) * math.log2(math.e)
    rows = min(ROWS, tokens * gs)
    parts = tokens * gs // rows

    def attend(i, src, own):
        keys = kvall[src, i, :, 0:att]
        values = jnp.concatenate([kvall[src, i, :, att:], jnp.ones((tokens, att), BF16)], axis=1)

        def part(p, c):
            span = pl.ds(pl.multiple_of(p * rows, rows), rows)
            weights = jnp.exp2(contract_lanes(qh[i, span, :], keys) * factor)
            if own:
                row = lax.broadcasted_iota(jnp.int32, (rows, tokens), 0) + p * rows
                col = lax.broadcasted_iota(jnp.int32, (rows, tokens), 1) * gs
                weights = jnp.where(row >= col, weights, 0.0)
            got = mm(weights.astype(BF16), values)
            acc[i, span, :] = got if own else acc[i, span, :] + got
            return c

        lax.fori_loop(0, parts, part, 0)

    for i in range(kvh):
        total = kvp[chan * kvh + i]
        for off in range(1, nx):
            cx = (mx + off) % nx
            chip_copy(i, cx, cx).wait_recv()
            total = total + r2[i, cx].astype(F32)
        key = total[:, 0:att]
        key = key * lax.rsqrt(jnp.mean(key * key, axis=-1, keepdims=True) + 1e-06)
        kvall[me, i, :, 0:att] = key.astype(BF16)
        kvall[me, i, :, att:] = total[:, att:].astype(BF16)

        @pl.when(me < nseq - 1)
        def _(i=i):
            kv_copy(me, i).start()

        attend(i, me, True)

    def earlier(s, c):
        src = me - s
        for i in range(kvh):
            kv_copy(src, i).wait_recv()

            @pl.when(me < nseq - 1)
            def _(i=i):
                kv_copy(src, i).start()

            attend(i, src, False)
        return c

    lax.fori_loop(1, me + 1, earlier, 0)

    out_rows = tokens // nch

    def finish(p, c):
        span = pl.ds(pl.multiple_of(p * out_rows * gs, out_rows * gs), out_rows * gs)
        done = [
            (acc[i, span, 0:att] / acc[i, span, att:]).reshape(out_rows, gs, att) for i in range(kvh)
        ]
        whole = done[0] if kvh == 1 else jnp.concatenate(done, axis=1)
        att_ref[pl.ds(p * out_rows, out_rows)] = whole.astype(BF16)
        return c

    lax.fori_loop(0, nch, finish, 0)

    for i in range(kvh):
        for off in range(nx):
            core_copy(i, (mx + off) % nx).wait_send()
        for off in range(1, nx):
            chip_copy(i, (mx + off) % nx, mx).wait_send()

    @pl.when(me < nseq - 1)
    def _():
        for copy in rim_copies():
            copy.wait_send()
        for j in range(nch):
            state_copy(j).wait_send()

        def sent(s, c):
            for i in range(kvh):
                kv_copy(s, i).wait_send()
            return c

        lax.fori_loop(0, me + 1, sent, 0)


def on_device(nseq, nchan, x_in, b_in, c_in, dt_in, a_log, z_in, conv_x, conv_bc, norm_gain, w_kv, queries):
    tokens, channels = x_in.shape
    _, ngroups, nstate = b_in.shape
    gn = ngroups * nstate
    heads = dt_in.shape[1]
    kv_heads, kw = w_kv.shape[1:]
    q_heads, att = queries.shape[1:]
    kvh = kv_heads // nchan
    gs = q_heads // kvh
    taps = conv_x.shape[0]
    cw = min(WIDE, channels // ngroups)
    nch = channels // cw
    nx = nchan // CORES
    bc = jnp.concatenate([b_in.reshape(tokens, gn), c_in.reshape(tokens, gn)], axis=1)
    tbc = jnp.concatenate([conv_bc[0].reshape(taps, gn), conv_bc[1].reshape(taps, gn)], axis=1)
    vmem = pl.BlockSpec(memory_space=pltpu.VMEM)
    hbm = pl.BlockSpec(memory_space=pl.ANY)
    dma = pltpu.SemaphoreType.DMA
    return pl.pallas_call(
        functools.partial(kernel, nseq, nchan, nstate, kv_heads),
        out_shape=(
            jax.ShapeDtypeStruct((tokens, channels), BF16),
            jax.ShapeDtypeStruct((tokens, q_heads, att), BF16),
        ),
        in_specs=[vmem] * 7 + [hbm] * 3,
        out_specs=(vmem, vmem),
        scratch_shapes=[
            pltpu.VMEM((tokens, channels), BF16),
            pltpu.VMEM((channels * kv_heads, kw), BF16),
            pltpu.VMEM((tokens, q_heads, att), BF16),
            pltpu.VMEM((RIM, channels), BF16),
            pltpu.VMEM((RIM, 2 * gn), BF16),
            pltpu.VMEM((tokens + 8, cw), F32),
            pltpu.VMEM((tokens + 8, 2 * gn), F32),
            pltpu.VMEM((tokens, 2 * gn), BF16),
            pltpu.VMEM((ngroups, tokens, tokens), BF16),
            pltpu.VMEM((4, tokens, heads), BF16),
            pltpu.VMEM((nch, tokens, cw), BF16),
            pltpu.VMEM((nch, nstate, cw), F32),
            pltpu.VMEM((nch, nstate, cw), BF16),
            pltpu.VMEM((nch, nstate, cw), BF16),
            pltpu.VMEM((nch, tokens, cw), F32),
            pltpu.VMEM((tokens, 128), F32),
            pltpu.VMEM((kv_heads, channels, kw), BF16),
            pltpu.VMEM((kv_heads, tokens, kw), F32),
            pltpu.VMEM((kvh, nx, tokens, kw), BF16),
            pltpu.VMEM((kvh, nx, tokens, kw), BF16),
            pltpu.VMEM((kvh, nx, tokens, kw), BF16),
            pltpu.VMEM((kvh, nx, tokens, kw), BF16),
            pltpu.VMEM((nseq, kvh, tokens, kw), BF16),
            pltpu.VMEM((kvh, tokens * gs, att), BF16),
            pltpu.VMEM((kvh, tokens * gs, 2 * att), F32),
            dma((3,)),
            dma((2,)),
            dma((2,)),
            dma((nch,)),
            dma((nch,)),
            dma((kvh, nx)),
            dma((kvh, nx)),
            dma((kvh, nx)),
            dma((kvh, nx)),
            dma((nseq, kvh)),
            dma((nseq, kvh)),
        ],
        compiler_params=pltpu.CompilerParams(
            collective_id=0, has_side_effects=True, vmem_limit_bytes=62 * 1024 * 1024
        ),
        name="mixer_attention",
    )(
        x_in, bc, dt_in, a_log.reshape(1, heads), conv_x, tbc, norm_gain.reshape(1, channels),
        z_in, w_kv.reshape(channels * kv_heads, kw), queries,
    )


def solution(mesh):
    return jax.shard_map(
        functools.partial(on_device, mesh.shape["seq"], mesh.shape["chan"]),
        mesh=mesh,
        in_specs=(
            P(("groups", "seq"), "chan"),
            P(("groups", "seq"), "chan", None),
            P(("groups", "seq"), "chan", None),
            P(("groups", "seq"), "chan"),
            P("chan"),
            P(("groups", "seq"), "chan"),
            P(None, "chan"),
            P(None, None, "chan", None),
            P("chan"),
            P("chan", None, None),
            P(("groups", "seq"), "chan", None),
        ),
        out_specs=(P(("groups", "seq"), "chan"), P(("groups", "seq"), "chan", None)),
        check_vma=False,
    )
```

time: 345 us -> 87.8 us (0.25); the launches traced: 341 us -> 87.5 us
  local copies, waits for them, and re-layouts: 124 us -> 7.38 us
  waiting for transfers between devices: 98.2 us -> 0 us
  Pallas kernels: 0 us -> 78.1 us
  matrix products: 66.3 us -> 0 us
  other arithmetic: 26.3 us -> 1.36 us
  between operations: 16 us -> 0.65 us
  blocking collectives: 8.58 us -> 0 us
    dynamic_update_slice x3 -> x0, local copies, waits for them, and re-layouts: 79.3 us -> none  [stretch_scan(): lax.scan(advance, initial, (to_blocks(x_heads), to_blocks(b_rows), to_blo...]
    pallas_call x0 -> x1, Pallas kernels: none -> 78.1 us  [on_device(): pl.pallas_call(functools.partial(kernel, nseq, nchan, nstate, kv_heads),...]
    dot_general x20 -> x0, matrix products: 66.3 us -> none  [the longest x3 16.6 us: advance(): within = jnp.einsum('tsgh,sghp->tghp', mixing, x_block, precision=HIGHEST)]
    all_gather x2 -> x0, waiting for transfers between devices: 59.2 us -> none  [the longest x1 30.2 us: on_device(): lax.all_gather(local_state[None].astype(jnp.bfloat16), 'seq', axis=0, til...]
    reduce_scatter x1 -> x0, waiting for transfers between devices: 39 us -> none  [on_device(): lax.psum_scatter(jnp.einsum('tc,chk->htk', mixer_out, w_kv, preferred_ele...]
    convert_element_type x11 -> x0, other arithmetic: 11.7 us -> none  [the longest x3 3.34 us: rounded(): return lax.optimization_barrier(values.astype(jnp.bfloat16))]
    all_gather x1 -> x0, blocking collectives: 8.58 us -> none  [on_device(): all_totals = lax.all_gather(totals[None], 'seq', axis=0, tiled=True)]
    mul x10 -> x0, local copies, waits for them, and re-layouts: 7.81 us -> none  [the longest x1 5.63 us: on_device(): grouped * grouped]
  transfers between devices with their start and end apart: 4 -> 0, of which waited for: 3 -> 0; matrix products, arithmetic and copies ran while one was open for 5% -> 0% of each run, Pallas kernels for 0% -> 0%
where the time goes in v1:
time: 87.8 us; the launch traced here: 87.5 us
  Pallas kernels  78.1 us (89%)
  local copies, waits for them, and re-layouts  7.38 us (8%)
  other arithmetic  1.36 us (2%)
    pallas_call x1, Pallas kernels, on_device(): pl.pallas_call(functools.partial(kernel, nseq, nchan, nstate, kv_heads),...  78.1 us
    unnamed x6, local copies, waits for them, and re-layouts  6.31 us

profile of v1, /device:TPU:24, one launch (start us, length us, event | category | flops | bytes accessed | tf_op | source)
XLA Modules:
  0.0 87.5 jit_solution(4808646661575591163)
XLA Ops:
  0.6 0.7 slice_bitcast_fusion.1
  1.3 0.6 pad_maximum_fusion.1.tbc_ref
  1.9 1.6 %copy.13.dt_ref = f32[384,32]{1,0:T(8,128)} copy(f32[384,32]{0,1:T(8,128)} %param.14) | data formatting | bytes 98304 | tf_op args[3]
  3.5 1.1 %copy_bitcast_fusion = (bf16[384,256]{1,0:T(8,128)(2,1)S(1)}, bf16[384,256]{1,0:T(8,128)(2,1)S(1)}) fusion(bf16[48,8,2,128]{3,2,1,0:T(2,128)(2,1)} %bitcast.20, bf16[48,8,2,128]{3,2,1,0:T(2,128)(2,1)} %bitcast.21), kind=kLoop, calls=%fused_computation.1 | loop fusion | bytes 786432 | tf_op jit(solution)/shard_map/reshape | solution.py:409
  4.6 0.8 pad_maximum_fusion.bc_ref
  5.4 78.1 %mixer_attention.1 = (bf16[384,2048]{1,0:T(8,128)(2,1)}, bf16[384,16,128]{2,1,0:T(8,128)(2,1)}) custom-call(bf16[384,2048]{1,0:T(8,128)(2,1)} %x_ref.1, bf16[384,512]{1,0:T(8,128)(2,1)} %pad_maximum_fusion.bc_ref, f32[384,32]{1,0:T(8,128)} %copy.13.dt_ref, f32[1,32]{1,0:T(1,128)} %bitcast.23, f32[4,2048]{1,0:T(4,128)} %tx_ref.1, ...), custom_call_target="tpu_custom_call" | custom-call | tf_op jit(solution)/shard_map/mixer_attention/pallas_call | solution.py:414
  83.5 0.0 copy-start
  83.5 2.8 %copy.24 = bf16[384,2048]{1,0:T(8,128)(2,1)} copy(bf16[384,2048]{1,0:T(8,128)(2,1)} %get-tuple-element.10) | data formatting | bytes 3145728
  86.4 0.0 copy-done
  86.4 1.1 %copy.25 = bf16[384,16,128]{2,1,0:T(8,128)(2,1)} copy(bf16[384,16,128]{2,1,0:T(8,128)(2,1)S(1)} %copy-done) | data formatting | bytes 3145728
  (1 shorter events, 0.0 us)
Async XLA Ops:
  83.5 2.9 %copy-start = (bf16[384,16,128]{2,1,0:T(8,128)(2,1)S(1)}, bf16[384,16,128]{2,1,0:T(8,128)(2,1)}, u32[]{:S(2)}) copy-start(bf16[384,16,128]{2,1,0:T(8,128)(2,1)} %get-tuple-element.11) | copy-start | bytes 4718596

commit v2 on v1

--- a/solution.py
+++ b/solution.py
@@ -40,18 +40,18 @@
 
 def kernel(
     nseq, nchan, nstate, kv_heads,
-    x_ref, bc_ref, dt_ref, alog_ref, tx_ref, tbc_ref, gain_ref, z_hbm, w_hbm, q_hbm,
+    x_ref, b_ref, c_ref, dt_ref, alog_ref, tx_ref, tbc_ref, gain_ref, z_hbm, w_hbm, q_hbm,
     mix_ref, att_ref,
-    zv, wv, qv, rimx, rimbc, xp, bcp, bcv, mask_cb, decay, xs, sl, sin, sout, ybuf, ssq,
+    zv, wv, qv, rimx, rimb, rimc, xp, bcp, bcv, mask_cb, decay, xs, sl, sin, sout, ybuf, ssq,
     wp, kvp, s1, r1, s2, r2, kvall, qh, acc,
     in_sem, rim_send, rim_recv, st_send, st_recv,
     c1_send, c1_recv, c2_send, c2_recv, kv_send, kv_recv,
 ):
     tokens, channels = x_ref.shape
-    heads = dt_ref.shape[1]
+    heads = dt_ref.shape[0]
     head_width = channels // heads
-    gn = bc_ref.shape[1] // 2
-    ngroups = gn // nstate
+    ngroups = b_ref.shape[1]
+    gn = ngroups * nstate
     nch, _, cw = xs.shape
     per = nch // ngroups
     chg = channels // ngroups
@@ -101,7 +101,8 @@
     def rim_copies():
         return (
             remote(x_ref.at[pl.ds(tokens - RIM, RIM)], rimx, rim_send.at[0], rim_recv.at[0], nxt),
-            remote(bc_ref.at[pl.ds(tokens - RIM, RIM)], rimbc, rim_send.at[1], rim_recv.at[1], nxt),
+            remote(b_ref.at[pl.ds(tokens - RIM, RIM)], rimb, rim_send.at[1], rim_recv.at[1], nxt),
+            remote(c_ref.at[pl.ds(tokens - RIM, RIM)], rimc, rim_send.at[2], rim_recv.at[2], nxt),
         )
 
     def state_copy(j):
@@ -118,11 +119,16 @@
     @pl.when(me == 0)
     def _():
         rimx[...] = jnp.zeros_like(rimx)
-        rimbc[...] = jnp.zeros_like(rimbc)
+        rimb[...] = jnp.zeros_like(rimb)
+        rimc[...] = jnp.zeros_like(rimc)
         sin[...] = jnp.zeros_like(sin)
 
     step = jnp.log(1.0 + jnp.exp(dt_ref[...]))
-    drop = -step * jnp.exp(alog_ref[...])
+    same = lax.broadcasted_iota(jnp.int32, (heads, heads), 0) == lax.broadcasted_iota(
+        jnp.int32, (heads, heads), 1
+    )
+    rates = jnp.sum(jnp.where(same, jnp.exp(alog_ref[...]), 0.0), axis=1, keepdims=True)
+    drop = -step * rates
     at_row = lax.broadcasted_iota(jnp.int32, (tokens, tokens), 0)
     at_col = lax.broadcasted_iota(jnp.int32, (tokens, tokens), 1)
     causal = at_row >= at_col
@@ -130,7 +136,7 @@
     d1, rest = split2(drop)
     d2 = rest
     d3 = (drop - d1.astype(F32) - d2.astype(F32)).astype(BF16)
-    running = mm(lower, d1) + mm(lower, d2) + mm(lower, d3)
+    running = contract_lanes(d1, lower) + contract_lanes(d2, lower) + contract_lanes(d3, lower)
     e_hi, e_lo = split2(jnp.exp(running))
     w_hi, w_lo = split2(jnp.exp(-running) * step)
     decay[0] = e_hi
@@ -148,12 +154,18 @@
         for copy in rim_copies():
             copy.wait_recv()
 
-    bcp[0:8, :] = rimbc[...].astype(F32)[8:16]
-    bcp[8 : 8 + tokens, :] = bc_ref[...].astype(F32)
-    summed = tbc_ref[0:1, :] * bcp[base : base + tokens, :]
-    for k in range(1, margin + 1):
-        summed = summed + tbc_ref[k : k + 1, :] * bcp[base + k : base + k + tokens, :]
-    bcv[...] = silu(summed).astype(BF16)
+    for which, (ref, rim) in enumerate(((b_ref, rimb), (c_ref, rimc))):
+        full = ref[...].astype(F32)
+        ahead = rim[...].astype(F32)
+        for g in range(ngroups):
+            lanes = slice(which * gn + g * nstate, which * gn + (g + 1) * nstate)
+            bcp[0:8, lanes] = ahead[8:16, g, :]
+            bcp[8 : 8 + tokens, lanes] = full[:, g, :]
+            summed = tbc_ref[which, 0, g : g + 1, :] * bcp[base : base + tokens, lanes]
+            for k in range(1, margin + 1):
+                taps = tbc_ref[which, k, g : g + 1, :]
+                summed = summed + taps * bcp[base + k : base + k + tokens, lanes]
+            bcv[:, lanes] = silu(summed).astype(BF16)
     for g in range(ngroups):
         cb = contract_lanes(
             bcv[:, gn + g * nstate : gn + (g + 1) * nstate], bcv[:, g * nstate : (g + 1) * nstate]
@@ -170,7 +182,7 @@
             total = total + tx_ref[k : k + 1, lanes] * xp[base + k : base + k + tokens, :]
         conv = silu(total).astype(BF16).astype(F32)
         each = spread(j)
-        scaled = (conv * (mm(decay[2], each) + mm(decay[3], each))).astype(BF16)
+        scaled = (conv * (contract_rows(decay[2], each) + contract_rows(decay[3], each))).astype(BF16)
         xs[j] = scaled
         own = contract_rows(bcv[:, pl.ds(pl.multiple_of(g * nstate, nstate), nstate)], scaled)
         sl[j] = own
@@ -184,8 +196,9 @@
 
     def last_decay(j):
         each = spread(j)
-        tail = pl.ds(tokens - RIM, RIM)
-        return (mm(decay[0, tail, :], each) + mm(decay[1, tail, :], each))[RIM - 1 : RIM, :]
+        tail = slice(tokens - 128, tokens)
+        got = contract_rows(decay[0, :, tail], each) + contract_rows(decay[1, :, tail], each)
+        return got[127:128, :]
 
     lax.fori_loop(0, nch, conv_chunk, 0)
 
@@ -201,14 +214,11 @@
     q_rows = tokens // nch
 
     def filler(j):
-        def one(n, c):
+        for n in range(w_parts):
             at = j * w_parts + n
             moved = mm(perm, wv[pl.ds(pl.multiple_of(at * WIDE, WIDE), WIDE), :]).astype(BF16)
             for h in range(kv_heads):
                 wp[h, pl.ds(pl.multiple_of(at * blk, blk), blk), :] = moved[h * blk : (h + 1) * blk]
-            return c
-
-        lax.fori_loop(0, w_parts, one, 0)
         qf = qv[pl.ds(j * q_rows, q_rows)].astype(F32)
         qn = qf * lax.rsqrt(jnp.mean(qf * qf, axis=-1, keepdims=True) + 1e-06)
         for i in range(kvh):
@@ -231,7 +241,7 @@
 
         filler(j)
         each = spread(j)
-        gate = silu(zv[:, lanes].astype(F32)) * (mm(decay[0], each) + mm(decay[1], each))
+        gate = silu(zv[:, lanes].astype(F32)) * (contract_rows(decay[0], each) + contract_rows(decay[1], each))
         c_rows = bcv[:, pl.ds(pl.multiple_of(gn + g * nstate, nstate), nstate)]
         y = (mm(mask_cb[g], xs[j]) + mm(c_rows, sin[j])) * gate
         ybuf[j] = y
@@ -248,6 +258,7 @@
         return got if g == 0 else kvp[h] + got
 
     ssq[...] = jnp.zeros_like(ssq)
+    acc[...] = jnp.zeros_like(acc)
     for g in range(ngroups):
         lax.fori_loop(g * per, (g + 1) * per, scan_chunk, 0)
         scale = lax.rsqrt(jnp.sum(ssq[...], axis=-1, keepdims=True) / chg + 1e-05)
@@ -288,7 +299,6 @@
             return c
 
         lax.fori_loop(0, nx, to_mate, 0)
-    for i in range(kvh):
 
         def to_chip(n, c, i=i):
             cx = (mx + 1 + n) % nx
@@ -323,11 +333,24 @@
                 col = lax.broadcasted_iota(jnp.int32, (rows, tokens), 1) * gs
                 weights = jnp.where(row >= col, weights, 0.0)
             got = mm(weights.astype(BF16), values)
-            acc[i, span, :] = got if own else acc[i, span, :] + got
+            acc[i, span, :] = acc[i, span, :] + got
             return c
 
         lax.fori_loop(0, parts, part, 0)
 
+    def earlier(src, c):
+        for i in range(kvh):
+            kv_copy(src, i).wait_recv()
+
+            @pl.when(me < nseq - 1)
+            def _(i=i):
+                kv_copy(src, i).start()
+
+            attend(i, src, False)
+        return c
+
+    before = jnp.minimum(me, max(nseq - 2, 0))
+    lax.fori_loop(0, before, earlier, 0)
     for i in range(kvh):
         total = kvp[chan * kvh + i]
         for off in range(1, nx):
@@ -344,20 +367,7 @@
             kv_copy(me, i).start()
 
         attend(i, me, True)
-
-    def earlier(s, c):
-        src = me - s
-        for i in range(kvh):
-            kv_copy(src, i).wait_recv()
-
-            @pl.when(me < nseq - 1)
-            def _(i=i):
-                kv_copy(src, i).start()
-
-            attend(i, src, False)
-        return c
-
-    lax.fori_loop(1, me + 1, earlier, 0)
+    lax.fori_loop(before, me, earlier, 0)
 
     out_rows = tokens // nch
 
@@ -402,12 +412,9 @@
     q_heads, att = queries.shape[1:]
     kvh = kv_heads // nchan
     gs = q_heads // kvh
-    taps = conv_x.shape[0]
     cw = min(WIDE, channels // ngroups)
     nch = channels // cw
     nx = nchan // CORES
-    bc = jnp.concatenate([b_in.reshape(tokens, gn), c_in.reshape(tokens, gn)], axis=1)
-    tbc = jnp.concatenate([conv_bc[0].reshape(taps, gn), conv_bc[1].reshape(taps, gn)], axis=1)
     vmem = pl.BlockSpec(memory_space=pltpu.VMEM)
     hbm = pl.BlockSpec(memory_space=pl.ANY)
     dma = pltpu.SemaphoreType.DMA
@@ -417,19 +424,20 @@
             jax.ShapeDtypeStruct((tokens, channels), BF16),
             jax.ShapeDtypeStruct((tokens, q_heads, att), BF16),
         ),
-        in_specs=[vmem] * 7 + [hbm] * 3,
+        in_specs=[vmem] * 8 + [hbm] * 3,
         out_specs=(vmem, vmem),
         scratch_shapes=[
             pltpu.VMEM((tokens, channels), BF16),
             pltpu.VMEM((channels * kv_heads, kw), BF16),
             pltpu.VMEM((tokens, q_heads, att), BF16),
             pltpu.VMEM((RIM, channels), BF16),
-            pltpu.VMEM((RIM, 2 * gn), BF16),
+            pltpu.VMEM((RIM, ngroups, nstate), BF16),
+            pltpu.VMEM((RIM, ngroups, nstate), BF16),
             pltpu.VMEM((tokens + 8, cw), F32),
             pltpu.VMEM((tokens + 8, 2 * gn), F32),
             pltpu.VMEM((tokens, 2 * gn), BF16),
             pltpu.VMEM((ngroups, tokens, tokens), BF16),
-            pltpu.VMEM((4, tokens, heads), BF16),
+            pltpu.VMEM((4, heads, tokens), BF16),
             pltpu.VMEM((nch, tokens, cw), BF16),
             pltpu.VMEM((nch, nstate, cw), F32),
             pltpu.VMEM((nch, nstate, cw), BF16),
@@ -446,8 +454,8 @@
             pltpu.VMEM((kvh, tokens * gs, att), BF16),
             pltpu.VMEM((kvh, tokens * gs, 2 * att), F32),
             dma((3,)),
-            dma((2,)),
-            dma((2,)),
+            dma((3,)),
+            dma((3,)),
             dma((nch,)),
             dma((nch,)),
             dma((kvh, nx)),
@@ -462,7 +470,7 @@
         ),
         name="mixer_attention",
     )(
-        x_in, bc, dt_in, a_log.reshape(1, heads), conv_x, tbc, norm_gain.reshape(1, channels),
+        x_in, b_in, c_in, dt_in.T, a_log.reshape(1, heads), conv_x, conv_bc, norm_gain.reshape(1, channels),
         z_in, w_kv.reshape(channels * kv_heads, kw), queries,
     )
 

time: 87.8 us -> 84.3 us (0.960)
  local copies, waits for them, and re-layouts: 7.38 us -> 3.99 us
  Pallas kernels: 78.1 us -> 79.5 us
  other arithmetic: 1.36 us -> 0 us
    unnamed x6 -> x4, local copies, waits for them, and re-layouts: 6.31 us -> 3.99 us
    pallas_call x1, Pallas kernels: 78.1 us -> 79.5 us  [on_device(): pl.pallas_call(functools.partial(kernel, nseq, nchan, nstate, kv_heads),...]
    concatenate x2 -> x0, other arithmetic: 1.36 us -> none  [the longest x1 0.78 us: on_device(): jnp.concatenate([b_in.reshape(tokens, gn), c_in.reshape(tokens, gn)], axi...]
    reshape x1 -> x0, local copies, waits for them, and re-layouts: 1.07 us -> none  [on_device(): c_in.reshape(tokens, gn)]
where the time goes in v2:
time: 84.3 us; the launch traced here: 84.2 us
  Pallas kernels  79.5 us (94%)
  local copies, waits for them, and re-layouts  3.99 us (5%)
    pallas_call x1, Pallas kernels, on_device(): pl.pallas_call(functools.partial(kernel, nseq, nchan, nstate, kv_heads),...  79.5 us
    unnamed x4, local copies, waits for them, and re-layouts  3.99 us

profile of v2, /device:TPU:24, one launch (start us, length us, event | category | flops | bytes accessed | tf_op | source)
XLA Modules:
  0.0 84.2 jit_solution(18211109514427310850)
XLA Ops:
  0.6 79.5 %mixer_attention.1 = (bf16[384,2048]{1,0:T(8,128)(2,1)}, bf16[384,16,128]{2,1,0:T(8,128)(2,1)}) custom-call(bf16[384,2048]{1,0:T(8,128)(2,1)} %x_ref.1, bf16[384,2,128]{2,1,0:T(2,128)(2,1)} %b_ref.1, bf16[384,2,128]{2,1,0:T(2,128)(2,1)} %c_ref.1, f32[32,384]{1,0:T(8,128)} %bitcast.5, f32[1,32]{1,0:T(1,128)} %bitcast.7, f32[4,2048]{1,0:T(4,128)} %tx_ref.1, ...), custom_call_target="tpu_custom_call" | custom-call | tf_op jit(solution)/shard_map/mixer_attention/pallas_call | solution.py:421
  80.2 0.0 copy-start
  80.2 2.8 %copy.15 = bf16[384,2048]{1,0:T(8,128)(2,1)} copy(bf16[384,2048]{1,0:T(8,128)(2,1)} %get-tuple-element.4) | data formatting | bytes 3145728
  83.0 0.0 copy-done
  83.0 1.1 %copy.16 = bf16[384,16,128]{2,1,0:T(8,128)(2,1)} copy(bf16[384,16,128]{2,1,0:T(8,128)(2,1)S(1)} %copy-done) | data formatting | bytes 3145728
Async XLA Ops:
  80.2 2.9 %copy-start = (bf16[384,16,128]{2,1,0:T(8,128)(2,1)S(1)}, bf16[384,16,128]{2,1,0:T(8,128)(2,1)}, u32[]{:S(2)}) copy-start(bf16[384,16,128]{2,1,0:T(8,128)(2,1)} %get-tuple-element.5) | copy-start | bytes 4718596

commit v3 on v2

--- a/solution.py
+++ b/solution.py
@@ -30,7 +30,8 @@
 
 
 def silu(v):
-    return v / (1.0 + jnp.exp(-v))
+    half = 0.5 * v
+    return half + half * jnp.tanh(half)
 
 
 def split2(v):
@@ -41,8 +42,8 @@
 def kernel(
     nseq, nchan, nstate, kv_heads,
     x_ref, b_ref, c_ref, dt_ref, alog_ref, tx_ref, tbc_ref, gain_ref, z_hbm, w_hbm, q_hbm,
-    mix_ref, att_ref,
-    zv, wv, qv, rimx, rimb, rimc, xp, bcp, bcv, mask_cb, decay, xs, sl, sin, sout, ybuf, ssq,
+    mix_out, att_ref,
+    mix_ref, zv, wv, qv, rimx, rimb, rimc, xp, bcp, bcv, mask_cb, decay, xs, sl, sin, sout, ybuf, ssq,
     wp, kvp, s1, r1, s2, r2, kvall, qh, acc,
     in_sem, rim_send, rim_recv, st_send, st_recv,
     c1_send, c1_recv, c2_send, c2_recv, kv_send, kv_recv,
@@ -172,25 +173,33 @@
         )
         mask_cb[g] = jnp.where(causal, cb, 0.0).astype(BF16)
 
-    def conv_chunk(j, c):
+    pair = 2 if per % 2 == 0 else 1
+
+    def conv_one(j, slot):
         lanes = pl.ds(pl.multiple_of(j * cw, cw), cw)
         g = j // per
-        xp[0:8, :] = rimx[:, lanes].astype(F32)[8:16]
-        xp[8 : 8 + tokens, :] = x_ref[:, lanes].astype(F32)
-        total = tx_ref[0:1, lanes] * xp[base : base + tokens, :]
+        xp[slot, 0:8, :] = rimx[:, lanes].astype(F32)[8:16]
+        xp[slot, 8 : 8 + tokens, :] = x_ref[:, lanes].astype(F32)
+        total = tx_ref[0:1, lanes] * xp[slot, base : base + tokens, :]
         for k in range(1, margin + 1):
-            total = total + tx_ref[k : k + 1, lanes] * xp[base + k : base + k + tokens, :]
+            total = total + tx_ref[k : k + 1, lanes] * xp[slot, base + k : base + k + tokens, :]
         conv = silu(total).astype(BF16).astype(F32)
         each = spread(j)
         scaled = (conv * (contract_rows(decay[2], each) + contract_rows(decay[3], each))).astype(BF16)
         xs[j] = scaled
         own = contract_rows(bcv[:, pl.ds(pl.multiple_of(g * nstate, nstate), nstate)], scaled)
-        sl[j] = own
+        sl[j] = own * last_decay(j)
+
+    def conv_chunks(p, c):
+        for k in range(pair):
+            conv_one(p * pair + k, k)
 
         @pl.when(me == 0)
         def _():
-            sout[j] = (own * last_decay(j)).astype(BF16)
-            state_copy(j).start()
+            for k in range(pair):
+                j = p * pair + k
+                sout[j] = sl[j].astype(BF16)
+                state_copy(j).start()
 
         return c
 
@@ -200,10 +209,9 @@
         got = contract_rows(decay[0, :, tail], each) + contract_rows(decay[1, :, tail], each)
         return got[127:128, :]
 
-    lax.fori_loop(0, nch, conv_chunk, 0)
+    lax.fori_loop(0, nch // pair, conv_chunks, 0)
 
     z_copy.wait()
-    q_copy.wait()
     w_copy.wait()
 
     blk = WIDE // kv_heads
@@ -213,12 +221,14 @@
     w_parts = channels // blk // nch
     q_rows = tokens // nch
 
-    def filler(j):
+    def weights_part(j):
         for n in range(w_parts):
             at = j * w_parts + n
             moved = mm(perm, wv[pl.ds(pl.multiple_of(at * WIDE, WIDE), WIDE), :]).astype(BF16)
             for h in range(kv_heads):
                 wp[h, pl.ds(pl.multiple_of(at * blk, blk), blk), :] = moved[h * blk : (h + 1) * blk]
+
+    def query_part(j, c):
         qf = qv[pl.ds(j * q_rows, q_rows)].astype(F32)
         qn = qf * lax.rsqrt(jnp.mean(qf * qf, axis=-1, keepdims=True) + 1e-06)
         for i in range(kvh):
@@ -226,30 +236,38 @@
                 qn[:, i * gs : (i + 1) * gs, :].reshape(q_rows * gs, att).astype(BF16)
             )
 
-    def scan_chunk(j, c):
-        lanes = pl.ds(pl.multiple_of(j * cw, cw), cw)
-        g = j // per
-
-        @pl.when(me > 0)
-        def _():
-            state_copy(j).wait_recv()
-
-        @pl.when((me > 0) & (me < nseq - 1))
-        def _():
-            sout[j] = ((sin[j].astype(F32) + sl[j]) * last_decay(j)).astype(BF16)
-            state_copy(j).start()
-
-        filler(j)
-        each = spread(j)
-        gate = silu(zv[:, lanes].astype(F32)) * (contract_rows(decay[0], each) + contract_rows(decay[1], each))
-        c_rows = bcv[:, pl.ds(pl.multiple_of(gn + g * nstate, nstate), nstate)]
-        y = (mm(mask_cb[g], xs[j]) + mm(c_rows, sin[j])) * gate
-        ybuf[j] = y
-        sq = y * y
-        part = sq[:, 0:128]
-        for k in range(1, cw // 128):
-            part = part + sq[:, k * 128 : (k + 1) * 128]
-        ssq[...] = part + jnp.where(j % per == 0, 0.0, ssq[...])
+        return c
+
+    def scan_chunks(p, c):
+        for k in range(pair):
+            j = p * pair + k
+
+            @pl.when(me > 0)
+            def _(j=j):
+                state_copy(j).wait_recv()
+
+            @pl.when((me > 0) & (me < nseq - 1))
+            def _(j=j):
+                sout[j] = (sin[j].astype(F32) * last_decay(j) + sl[j]).astype(BF16)
+                state_copy(j).start()
+
+        sums = jnp.where((p * pair) % per == 0, 0.0, ssq[...])
+        for k in range(pair):
+            j = p * pair + k
+            lanes = pl.ds(pl.multiple_of(j * cw, cw), cw)
+            g = j // per
+            weights_part(j)
+            each = spread(j)
+            gate = silu(zv[:, lanes].astype(F32)) * (
+                contract_rows(decay[0], each) + contract_rows(decay[1], each)
+            )
+            c_rows = bcv[:, pl.ds(pl.multiple_of(gn + g * nstate, nstate), nstate)]
+            y = (mm(mask_cb[g], xs[j]) + mm(c_rows, sin[j])) * gate
+            ybuf[j] = y
+            sq = y * y
+            for m in range(cw // 128):
+                sums = sums + sq[:, m * 128 : (m + 1) * 128]
+        ssq[...] = sums
         return c
 
     def kv_dot(g, h):
@@ -258,9 +276,8 @@
         return got if g == 0 else kvp[h] + got
 
     ssq[...] = jnp.zeros_like(ssq)
-    acc[...] = jnp.zeros_like(acc)
     for g in range(ngroups):
-        lax.fori_loop(g * per, (g + 1) * per, scan_chunk, 0)
+        lax.fori_loop(g * per // pair, (g + 1) * per // pair, scan_chunks, 0)
         scale = lax.rsqrt(jnp.sum(ssq[...], axis=-1, keepdims=True) / chg + 1e-05)
 
         def norm_chunk(j, c):
@@ -276,6 +293,9 @@
                 return c
 
             lax.fori_loop(0, kv_heads, kv_part, 0)
+
+    mix_copy = pltpu.make_async_copy(mix_ref, mix_out, in_sem.at[3])
+    mix_copy.start()
 
     last = ngroups - 1
 
@@ -333,12 +353,13 @@
                 col = lax.broadcasted_iota(jnp.int32, (rows, tokens), 1) * gs
                 weights = jnp.where(row >= col, weights, 0.0)
             got = mm(weights.astype(BF16), values)
-            acc[i, span, :] = acc[i, span, :] + got
+            acc[i, span, :] = got if own else acc[i, span, :] + got
             return c
 
         lax.fori_loop(0, parts, part, 0)
 
-    def earlier(src, c):
+    def earlier(back, c):
+        src = me - back
         for i in range(kvh):
             kv_copy(src, i).wait_recv()
 
@@ -349,8 +370,8 @@
             attend(i, src, False)
         return c
 
-    before = jnp.minimum(me, max(nseq - 2, 0))
-    lax.fori_loop(0, before, earlier, 0)
+    q_copy.wait()
+    lax.fori_loop(0, nch, query_part, 0)
     for i in range(kvh):
         total = kvp[chan * kvh + i]
         for off in range(1, nx):
@@ -367,7 +388,7 @@
             kv_copy(me, i).start()
 
         attend(i, me, True)
-    lax.fori_loop(before, me, earlier, 0)
+    lax.fori_loop(1, me + 1, earlier, 0)
 
     out_rows = tokens // nch
 
@@ -382,6 +403,7 @@
 
     lax.fori_loop(0, nch, finish, 0)
 
+    mix_copy.wait()
     for i in range(kvh):
         for off in range(nx):
             core_copy(i, (mx + off) % nx).wait_send()
@@ -425,15 +447,16 @@
             jax.ShapeDtypeStruct((tokens, q_heads, att), BF16),
         ),
         in_specs=[vmem] * 8 + [hbm] * 3,
-        out_specs=(vmem, vmem),
+        out_specs=(hbm, vmem),
         scratch_shapes=[
+            pltpu.VMEM((tokens, channels), BF16),
             pltpu.VMEM((tokens, channels), BF16),
             pltpu.VMEM((channels * kv_heads, kw), BF16),
             pltpu.VMEM((tokens, q_heads, att), BF16),
             pltpu.VMEM((RIM, channels), BF16),
             pltpu.VMEM((RIM, ngroups, nstate), BF16),
             pltpu.VMEM((RIM, ngroups, nstate), BF16),
-            pltpu.VMEM((tokens + 8, cw), F32),
+            pltpu.VMEM((2, tokens + 8, cw), F32),
             pltpu.VMEM((tokens + 8, 2 * gn), F32),
             pltpu.VMEM((tokens, 2 * gn), BF16),
             pltpu.VMEM((ngroups, tokens, tokens), BF16),
@@ -453,7 +476,7 @@
             pltpu.VMEM((nseq, kvh, tokens, kw), BF16),
             pltpu.VMEM((kvh, tokens * gs, att), BF16),
             pltpu.VMEM((kvh, tokens * gs, 2 * att), F32),
-            dma((3,)),
+            dma((4,)),
             dma((3,)),
             dma((3,)),
             dma((nch,)),

time: 84.3 us -> 76 us (0.902)
  Pallas kernels: 79.5 us -> 70.9 us
    pallas_call x1, Pallas kernels: 79.5 us -> 70.9 us  [on_device(): pl.pallas_call(functools.partial(kernel, nseq, nchan, nstate, kv_heads),...]
where the time goes in v3:
time: 76 us; the launch traced here: 75.6 us
  Pallas kernels  70.9 us (93%)
  local copies, waits for them, and re-layouts  3.99 us (5%)
    pallas_call x1, Pallas kernels, on_device(): pl.pallas_call(functools.partial(kernel, nseq, nchan, nstate, kv_heads),...  70.9 us
    unnamed x4, local copies, waits for them, and re-layouts  3.99 us

profile of v3, /device:TPU:24, one launch (start us, length us, event | category | flops | bytes accessed | tf_op | source)
XLA Modules:
  0.0 75.6 jit_solution(8022919871179815836)
XLA Ops:
  0.6 70.9 %mixer_attention.1 = (bf16[384,2048]{1,0:T(8,128)(2,1)}, bf16[384,16,128]{2,1,0:T(8,128)(2,1)}) custom-call(bf16[384,2048]{1,0:T(8,128)(2,1)} %x_ref.1, bf16[384,2,128]{2,1,0:T(2,128)(2,1)} %b_ref.1, bf16[384,2,128]{2,1,0:T(2,128)(2,1)} %c_ref.1, f32[32,384]{1,0:T(8,128)} %bitcast.5, f32[1,32]{1,0:T(1,128)} %bitcast.7, f32[4,2048]{1,0:T(4,128)} %tx_ref.1, ...), custom_call_target="tpu_custom_call" | custom-call | tf_op jit(solution)/shard_map/mixer_attention/pallas_call | solution.py:443
  71.6 0.0 copy-start
  71.6 2.8 %copy.15 = bf16[384,2048]{1,0:T(8,128)(2,1)} copy(bf16[384,2048]{1,0:T(8,128)(2,1)} %get-tuple-element.4) | data formatting | bytes 3145728
  74.4 0.0 copy-done
  74.4 1.1 %copy.16 = bf16[384,16,128]{2,1,0:T(8,128)(2,1)} copy(bf16[384,16,128]{2,1,0:T(8,128)(2,1)S(1)} %copy-done) | data formatting | bytes 3145728
Async XLA Ops:
  71.6 2.9 %copy-start = (bf16[384,16,128]{2,1,0:T(8,128)(2,1)S(1)}, bf16[384,16,128]{2,1,0:T(8,128)(2,1)}, u32[]{:S(2)}) copy-start(bf16[384,16,128]{2,1,0:T(8,128)(2,1)} %get-tuple-element.5) | copy-start | bytes 4718596

commit v4 on v3

--- a/solution.py
+++ b/solution.py
@@ -15,6 +15,8 @@
 CORES = 2
 WIDE = 256
 ROWS = 512
+HALVES = 2
+OUT_PARTS = 4
 
 
 def mm(a, b):
@@ -109,8 +111,10 @@
     def state_copy(j):
         return remote(sout.at[j], sin.at[j], st_send.at[j], st_recv.at[j], nxt)
 
-    def kv_copy(src, i):
-        return remote(kvall.at[src, i], kvall.at[src, i], kv_send.at[src, i], kv_recv.at[src, i], nxt)
+    def kv_copy(src, i, f):
+        half = tokens // HALVES
+        block = kvall.at[src, i, pl.ds(f * half, half)]
+        return remote(block, block, kv_send.at[src, i, f], kv_recv.at[src, i, f], nxt)
 
     @pl.when(me < nseq - 1)
     def _():
@@ -190,6 +194,19 @@
         own = contract_rows(bcv[:, pl.ds(pl.multiple_of(g * nstate, nstate), nstate)], scaled)
         sl[j] = own * last_decay(j)
 
+    pairs = nch // pair
+    ahead_by = 2
+
+    def take_states(p):
+        for k in range(pair):
+            j = p * pair + k
+            state_copy(j).wait_recv()
+
+            @pl.when(me < nseq - 1)
+            def _(j=j):
+                sout[j] = (sin[j].astype(F32) * last_decay(j) + sl[j]).astype(BF16)
+                state_copy(j).start()
+
     def conv_chunks(p, c):
         for k in range(pair):
             conv_one(p * pair + k, k)
@@ -200,6 +217,10 @@
                 j = p * pair + k
                 sout[j] = sl[j].astype(BF16)
                 state_copy(j).start()
+
+        @pl.when((me == 1) & (p >= ahead_by))
+        def _():
+            take_states(p - ahead_by)
 
         return c
 
@@ -239,17 +260,9 @@
         return c
 
     def scan_chunks(p, c):
-        for k in range(pair):
-            j = p * pair + k
-
-            @pl.when(me > 0)
-            def _(j=j):
-                state_copy(j).wait_recv()
-
-            @pl.when((me > 0) & (me < nseq - 1))
-            def _(j=j):
-                sout[j] = (sin[j].astype(F32) * last_decay(j) + sl[j]).astype(BF16)
-                state_copy(j).start()
+        @pl.when((me > 1) | ((me == 1) & (p >= pairs - ahead_by)))
+        def _():
+            take_states(p)
 
         sums = jnp.where((p * pair) % per == 0, 0.0, ssq[...])
         for k in range(pair):
@@ -304,9 +317,12 @@
             s1.at[i, cx], r1.at[i, cx], c1_send.at[i, cx], c1_recv.at[i, cx], {"chan": mate_id}
         )
 
-    def chip_copy(i, to, slot):
+    half = tokens // HALVES
+
+    def chip_copy(i, to, slot, f):
+        span = pl.ds(f * half, half)
         return remote(
-            s2.at[i, to], r2.at[i, slot], c2_send.at[i, to], c2_recv.at[i, slot],
+            s2.at[i, to, span], r2.at[i, slot, span], c2_send.at[i, to, f], c2_recv.at[i, slot, f],
             {"chan": to * CORES + core},
         )
 
@@ -331,7 +347,8 @@
             @pl.when(n < nx - 1)
             def _():
                 s2[i, cx] = both.astype(BF16)
-                chip_copy(i, cx, mx).start()
+                for f in range(HALVES):
+                    chip_copy(i, cx, mx, f).start()
 
             return c
 
@@ -358,57 +375,71 @@
 
         lax.fori_loop(0, parts, part, 0)
 
+    out_rows = tokens // nch
+
+    def finish(i):
+        def part(p, c):
+            span = pl.ds(pl.multiple_of(p * out_rows * gs, out_rows * gs), out_rows * gs)
+            done = acc[i, span, 0:att] / acc[i, span, att:]
+            att_ref[pl.ds(p * out_rows, out_rows), i * gs : (i + 1) * gs, :] = done.astype(
+                BF16
+            ).reshape(out_rows, gs, att)
+            return c
+
+        lax.fori_loop(0, nch, part, 0)
+
     def earlier(back, c):
         src = me - back
         for i in range(kvh):
-            kv_copy(src, i).wait_recv()
-
-            @pl.when(me < nseq - 1)
+            for f in range(HALVES):
+                kv_copy(src, i, f).wait_recv()
+
+                @pl.when(me < nseq - 1)
+                def _(i=i, f=f):
+                    kv_copy(src, i, f).start()
+
+            attend(i, src, False)
+
+            @pl.when(back == me)
             def _(i=i):
-                kv_copy(src, i).start()
-
-            attend(i, src, False)
+                finish(i)
+
         return c
 
     q_copy.wait()
     lax.fori_loop(0, nch, query_part, 0)
     for i in range(kvh):
-        total = kvp[chan * kvh + i]
-        for off in range(1, nx):
-            cx = (mx + off) % nx
-            chip_copy(i, cx, cx).wait_recv()
-            total = total + r2[i, cx].astype(F32)
-        key = total[:, 0:att]
-        key = key * lax.rsqrt(jnp.mean(key * key, axis=-1, keepdims=True) + 1e-06)
-        kvall[me, i, :, 0:att] = key.astype(BF16)
-        kvall[me, i, :, att:] = total[:, att:].astype(BF16)
-
-        @pl.when(me < nseq - 1)
+        for f in range(HALVES):
+            span = slice(f * half, (f + 1) * half)
+            total = kvp[chan * kvh + i, span]
+            for off in range(1, nx):
+                cx = (mx + off) % nx
+                chip_copy(i, cx, cx, f).wait_recv()
+                total = total + r2[i, cx, span].astype(F32)
+            key = total[:, 0:att]
+            key = key * lax.rsqrt(jnp.mean(key * key, axis=-1, keepdims=True) + 1e-06)
+            kvall[me, i, span, 0:att] = key.astype(BF16)
+            kvall[me, i, span, att:] = total[:, att:].astype(BF16)
+
+            @pl.when(me < nseq - 1)
+            def _(i=i, f=f):
+                kv_copy(me, i, f).start()
+
+        attend(i, me, True)
+
+        @pl.when(me == 0)
         def _(i=i):
-            kv_copy(me, i).start()
-
-        attend(i, me, True)
+            finish(i)
+
     lax.fori_loop(1, me + 1, earlier, 0)
-
-    out_rows = tokens // nch
-
-    def finish(p, c):
-        span = pl.ds(pl.multiple_of(p * out_rows * gs, out_rows * gs), out_rows * gs)
-        done = [
-            (acc[i, span, 0:att] / acc[i, span, att:]).reshape(out_rows, gs, att) for i in range(kvh)
-        ]
-        whole = done[0] if kvh == 1 else jnp.concatenate(done, axis=1)
-        att_ref[pl.ds(p * out_rows, out_rows)] = whole.astype(BF16)
-        return c
-
-    lax.fori_loop(0, nch, finish, 0)
 
     mix_copy.wait()
     for i in range(kvh):
         for off in range(nx):
             core_copy(i, (mx + off) % nx).wait_send()
         for off in range(1, nx):
-            chip_copy(i, (mx + off) % nx, mx).wait_send()
+            for f in range(HALVES):
+                chip_copy(i, (mx + off) % nx, mx, f).wait_send()
 
     @pl.when(me < nseq - 1)
     def _():
@@ -419,10 +450,24 @@
 
         def sent(s, c):
             for i in range(kvh):
-                kv_copy(s, i).wait_send()
+                for f in range(HALVES):
+                    kv_copy(s, i, f).wait_send()
             return c
 
         lax.fori_loop(0, me + 1, sent, 0)
+
+
+def hand_out(a_in, b_in, a_out, b_out, sem):
+    rows = a_in.shape[0] // OUT_PARTS
+    copies = []
+    for n in range(OUT_PARTS):
+        span = pl.ds(n * rows, rows)
+        copies.append(pltpu.make_async_copy(a_in.at[span], a_out.at[span], sem.at[0, n]))
+        copies.append(pltpu.make_async_copy(b_in.at[span], b_out.at[span], sem.at[1, n]))
+    for copy in copies:
+        copy.start()
+    for copy in copies:
+        copy.wait()
 
 
 def on_device(nseq, nchan, x_in, b_in, c_in, dt_in, a_log, z_in, conv_x, conv_bc, norm_gain, w_kv, queries):
@@ -440,7 +485,7 @@
     vmem = pl.BlockSpec(memory_space=pltpu.VMEM)
     hbm = pl.BlockSpec(memory_space=pl.ANY)
     dma = pltpu.SemaphoreType.DMA
-    return pl.pallas_call(
+    mixed, attended = pl.pallas_call(
         functools.partial(kernel, nseq, nchan, nstate, kv_heads),
         out_shape=(
             jax.ShapeDtypeStruct((tokens, channels), BF16),
@@ -483,10 +528,10 @@
             dma((nch,)),
             dma((kvh, nx)),
             dma((kvh, nx)),
-            dma((kvh, nx)),
-            dma((kvh, nx)),
-            dma((nseq, kvh)),
-            dma((nseq, kvh)),
+            dma((kvh, nx, HALVES)),
+            dma((kvh, nx, HALVES)),
+            dma((nseq, kvh, HALVES)),
+            dma((nseq, kvh, HALVES)),
         ],
         compiler_params=pltpu.CompilerParams(
             collective_id=0, has_side_effects=True, vmem_limit_bytes=62 * 1024 * 1024
@@ -496,6 +541,18 @@
         x_in, b_in, c_in, dt_in.T, a_log.reshape(1, heads), conv_x, conv_bc, norm_gain.reshape(1, channels),
         z_in, w_kv.reshape(channels * kv_heads, kw), queries,
     )
+    return pl.pallas_call(
+        hand_out,
+        out_shape=(
+            jax.ShapeDtypeStruct((tokens, channels), BF16),
+            jax.ShapeDtypeStruct((tokens, q_heads, att), BF16),
+        ),
+        in_specs=[hbm, hbm],
+        out_specs=(hbm, hbm),
+        scratch_shapes=[dma((2, OUT_PARTS))],
+        compiler_params=pltpu.CompilerParams(vmem_limit_bytes=62 * 1024 * 1024),
+        name="hand_out",
+    )(mixed, attended)
 
 
 def solution(mesh):

time: 76 us -> 169 us (2.22)
  Pallas kernels: 70.9 us -> 168 us
  local copies, waits for them, and re-layouts: 3.99 us -> 0 us
    pallas_call x0 -> x1, Pallas kernels: none -> 96.5 us  [on_device(): pl.pallas_call(hand_out, out_shape=(jax.ShapeDtypeStruct((tokens, channel...]
    unnamed x4 -> x0, local copies, waits for them, and re-layouts: 3.99 us -> none
where the time goes in v4:
time: 169 us; the launch traced here: 168 us
  Pallas kernels  168 us (99%)
    pallas_call x1, Pallas kernels, on_device(): pl.pallas_call(hand_out, out_shape=(jax.ShapeDtypeStruct((tokens, channel...  96.5 us
    pallas_call x1, Pallas kernels, on_device(): pl.pallas_call(functools.partial(kernel, nseq, nchan, nstate, kv_heads),...  71.1 us

profile of v4, /device:TPU:24, one launch (start us, length us, event | category | flops | bytes accessed | tf_op | source)
XLA Modules:
  0.0 168.3 jit_solution(2956737425065872627)
XLA Ops:
  0.6 71.1 %mixer_attention.1 = (bf16[384,2048]{1,0:T(8,128)(2,1)}, bf16[384,16,128]{2,1,0:T(8,128)(2,1)}) custom-call(bf16[384,2048]{1,0:T(8,128)(2,1)} %x_ref.1, bf16[384,2,128]{2,1,0:T(2,128)(2,1)} %b_ref.1, bf16[384,2,128]{2,1,0:T(2,128)(2,1)} %c_ref.1, f32[32,384]{1,0:T(8,128)} %bitcast.5, f32[1,32]{1,0:T(1,128)} %bitcast.7, f32[4,2048]{1,0:T(4,128)} %tx_ref.1, ...), custom_call_target="tpu_custom_call" | custom-call | tf_op jit(solution)/shard_map/mixer_attention/pallas_call | solution.py:488
  71.8 96.5 %hand_out.1 = (bf16[384,2048]{1,0:T(8,128)(2,1)}, bf16[384,16,128]{2,1,0:T(8,128)(2,1)}) custom-call(bf16[384,2048]{1,0:T(8,128)(2,1)} %get-tuple-element.4.a_in, bf16[384,16,128]{2,1,0:T(8,128)(2,1)} %get-tuple-element.5.b_in), custom_call_target="tpu_custom_call" | custom-call | tf_op jit(solution)/shard_map/hand_out/pallas_call | solution.py:544

commit v5 on v4

--- a/solution.py
+++ b/solution.py
@@ -359,21 +359,18 @@
     parts = tokens * gs // rows
 
     def attend(i, src, own):
-        keys = kvall[src, i, :, 0:att]
-        values = jnp.concatenate([kvall[src, i, :, att:], jnp.ones((tokens, att), BF16)], axis=1)
-
-        def part(p, c):
-            span = pl.ds(pl.multiple_of(p * rows, rows), rows)
+        for p in range(parts):
+            span = slice(p * rows, (p + 1) * rows)
+            seen = min(tokens, -(-(p + 1) * rows // (gs * 128)) * 128) if own else tokens
+            keys = kvall[src, i, 0:seen, 0:att]
+            values = jnp.concatenate([kvall[src, i, 0:seen, att:], jnp.ones((seen, att), BF16)], axis=1)
             weights = jnp.exp2(contract_lanes(qh[i, span, :], keys) * factor)
             if own:
-                row = lax.broadcasted_iota(jnp.int32, (rows, tokens), 0) + p * rows
-                col = lax.broadcasted_iota(jnp.int32, (rows, tokens), 1) * gs
+                row = lax.broadcasted_iota(jnp.int32, (rows, seen), 0) + p * rows
+                col = lax.broadcasted_iota(jnp.int32, (rows, seen), 1) * gs
                 weights = jnp.where(row >= col, weights, 0.0)
             got = mm(weights.astype(BF16), values)
             acc[i, span, :] = got if own else acc[i, span, :] + got
-            return c
-
-        lax.fori_loop(0, parts, part, 0)
 
     out_rows = tokens // nch
 
@@ -457,17 +454,21 @@
         lax.fori_loop(0, me + 1, sent, 0)
 
 
-def hand_out(a_in, b_in, a_out, b_out, sem):
+def hand_out(a_in, b_in, a_out, b_out, a_mid, b_mid, sem_in, sem_out):
     rows = a_in.shape[0] // OUT_PARTS
-    copies = []
+    reads, writes = [], []
     for n in range(OUT_PARTS):
         span = pl.ds(n * rows, rows)
-        copies.append(pltpu.make_async_copy(a_in.at[span], a_out.at[span], sem.at[0, n]))
-        copies.append(pltpu.make_async_copy(b_in.at[span], b_out.at[span], sem.at[1, n]))
-    for copy in copies:
-        copy.start()
-    for copy in copies:
-        copy.wait()
+        for k, (src, mid, dst) in enumerate(((a_in, a_mid, a_out), (b_in, b_mid, b_out))):
+            reads.append(pltpu.make_async_copy(src.at[span], mid.at[span], sem_in.at[k, n]))
+            writes.append(pltpu.make_async_copy(mid.at[span], dst.at[span], sem_out.at[k, n]))
+    for read in reads:
+        read.start()
+    for read, write in zip(reads, writes):
+        read.wait()
+        write.start()
+    for write in writes:
+        write.wait()
 
 
 def on_device(nseq, nchan, x_in, b_in, c_in, dt_in, a_log, z_in, conv_x, conv_bc, norm_gain, w_kv, queries):
@@ -549,7 +550,12 @@
         ),
         in_specs=[hbm, hbm],
         out_specs=(hbm, hbm),
-        scratch_shapes=[dma((2, OUT_PARTS))],
+        scratch_shapes=[
+            pltpu.VMEM((tokens, channels), BF16),
+            pltpu.VMEM((tokens, q_heads, att), BF16),
+            dma((2, OUT_PARTS)),
+            dma((2, OUT_PARTS)),
+        ],
         compiler_params=pltpu.CompilerParams(vmem_limit_bytes=62 * 1024 * 1024),
         name="hand_out",
     )(mixed, attended)

time: 169 us -> 69.8 us (0.41)
  Pallas kernels: 168 us -> 68.8 us
    pallas_call x1, Pallas kernels: 96.5 us -> 2.79 us  [on_device(): pl.pallas_call(hand_out, out_shape=(jax.ShapeDtypeStruct((tokens, channel...]
    pallas_call x1, Pallas kernels: 71.1 us -> 66.1 us  [on_device(): pl.pallas_call(functools.partial(kernel, nseq, nchan, nstate, kv_heads),...]
where the time goes in v5:
time: 69.8 us; the launch traced here: 69.6 us
  Pallas kernels  68.8 us (99%)
  between operations  0.8 us (1%)
    pallas_call x1, Pallas kernels, on_device(): pl.pallas_call(functools.partial(kernel, nseq, nchan, nstate, kv_heads),...  66.1 us
    pallas_call x1, Pallas kernels, on_device(): pl.pallas_call(hand_out, out_shape=(jax.ShapeDtypeStruct((tokens, channel...  2.79 us

profile of v5, /device:TPU:24, one launch (start us, length us, event | category | flops | bytes accessed | tf_op | source)
XLA Modules:
  0.0 69.6 jit_solution(10070912317627205090)
XLA Ops:
  0.6 66.1 %mixer_attention.1 = (bf16[384,2048]{1,0:T(8,128)(2,1)}, bf16[384,16,128]{2,1,0:T(8,128)(2,1)}) custom-call(bf16[384,2048]{1,0:T(8,128)(2,1)} %x_ref.1, bf16[384,2,128]{2,1,0:T(2,128)(2,1)} %b_ref.1, bf16[384,2,128]{2,1,0:T(2,128)(2,1)} %c_ref.1, f32[32,384]{1,0:T(8,128)} %bitcast.5, f32[1,32]{1,0:T(1,128)} %bitcast.7, f32[4,2048]{1,0:T(4,128)} %tx_ref.1, ...), custom_call_target="tpu_custom_call" | custom-call | tf_op jit(solution)/shard_map/mixer_attention/pallas_call | solution.py:489
  66.7 2.8 %hand_out.1 = (bf16[384,2048]{1,0:T(8,128)(2,1)}, bf16[384,16,128]{2,1,0:T(8,128)(2,1)}) custom-call(bf16[384,2048]{1,0:T(8,128)(2,1)} %get-tuple-element.4.a_in, bf16[384,16,128]{2,1,0:T(8,128)(2,1)} %get-tuple-element.5.b_in), custom_call_target="tpu_custom_call" | custom-call | tf_op jit(solution)/shard_map/hand_out/pallas_call | solution.py:545

commit v6 on v5

--- a/solution.py
+++ b/solution.py
@@ -15,7 +15,7 @@
 CORES = 2
 WIDE = 256
 ROWS = 512
-HALVES = 2
+HALVES = 4
 OUT_PARTS = 4
 
 
@@ -159,7 +159,7 @@
         for copy in rim_copies():
             copy.wait_recv()
 
-    for which, (ref, rim) in enumerate(((b_ref, rimb), (c_ref, rimc))):
+    def conv_bc(which, ref, rim):
         full = ref[...].astype(F32)
         ahead = rim[...].astype(F32)
         for g in range(ngroups):
@@ -171,11 +171,8 @@
                 taps = tbc_ref[which, k, g : g + 1, :]
                 summed = summed + taps * bcp[base + k : base + k + tokens, lanes]
             bcv[:, lanes] = silu(summed).astype(BF16)
-    for g in range(ngroups):
-        cb = contract_lanes(
-            bcv[:, gn + g * nstate : gn + (g + 1) * nstate], bcv[:, g * nstate : (g + 1) * nstate]
-        )
-        mask_cb[g] = jnp.where(causal, cb, 0.0).astype(BF16)
+
+    conv_bc(0, b_ref, rimb)
 
     pair = 2 if per % 2 == 0 else 1
 
@@ -231,6 +228,13 @@
         return got[127:128, :]
 
     lax.fori_loop(0, nch // pair, conv_chunks, 0)
+
+    conv_bc(1, c_ref, rimc)
+    for g in range(ngroups):
+        cb = contract_lanes(
+            bcv[:, gn + g * nstate : gn + (g + 1) * nstate], bcv[:, g * nstate : (g + 1) * nstate]
+        )
+        mask_cb[g] = jnp.where(causal, cb, 0.0).astype(BF16)
 
     z_copy.wait()
     w_copy.wait()
@@ -403,8 +407,6 @@
 
         return c
 
-    q_copy.wait()
-    lax.fori_loop(0, nch, query_part, 0)
     for i in range(kvh):
         for f in range(HALVES):
             span = slice(f * half, (f + 1) * half)
@@ -422,6 +424,9 @@
             def _(i=i, f=f):
                 kv_copy(me, i, f).start()
 
+        if i == 0:
+            q_copy.wait()
+            lax.fori_loop(0, nch, query_part, 0)
         attend(i, me, True)
 
         @pl.when(me == 0)

time: 69.8 us -> 71.3 us (1.021)
  Pallas kernels: 68.8 us -> 70.3 us
    pallas_call x1, Pallas kernels: 66.1 us -> 67.6 us  [on_device(): pl.pallas_call(functools.partial(kernel, nseq, nchan, nstate, kv_heads),...]
where the time goes in v6:
time: 71.3 us; the launch traced here: 71.1 us
  Pallas kernels  70.3 us (99%)
  between operations  0.8 us (1%)
    pallas_call x1, Pallas kernels, on_device(): pl.pallas_call(functools.partial(kernel, nseq, nchan, nstate, kv_heads),...  67.6 us
    pallas_call x1, Pallas kernels, on_device(): pl.pallas_call(hand_out, out_shape=(jax.ShapeDtypeStruct((tokens, channel...  2.79 us

profile of v6, /device:TPU:24, one launch (start us, length us, event | category | flops | bytes accessed | tf_op | source)
XLA Modules:
  0.0 71.1 jit_solution(9849664293452785872)
XLA Ops:
  0.6 67.6 %mixer_attention.1 = (bf16[384,2048]{1,0:T(8,128)(2,1)}, bf16[384,16,128]{2,1,0:T(8,128)(2,1)}) custom-call(bf16[384,2048]{1,0:T(8,128)(2,1)} %x_ref.1, bf16[384,2,128]{2,1,0:T(2,128)(2,1)} %b_ref.1, bf16[384,2,128]{2,1,0:T(2,128)(2,1)} %c_ref.1, f32[32,384]{1,0:T(8,128)} %bitcast.5, f32[1,32]{1,0:T(1,128)} %bitcast.7, f32[4,2048]{1,0:T(4,128)} %tx_ref.1, ...), custom_call_target="tpu_custom_call" | custom-call | tf_op jit(solution)/shard_map/mixer_attention/pallas_call | solution.py:494
  68.2 2.8 %hand_out.1 = (bf16[384,2048]{1,0:T(8,128)(2,1)}, bf16[384,16,128]{2,1,0:T(8,128)(2,1)}) custom-call(bf16[384,2048]{1,0:T(8,128)(2,1)} %get-tuple-element.4.a_in, bf16[384,16,128]{2,1,0:T(8,128)(2,1)} %get-tuple-element.5.b_in), custom_call_target="tpu_custom_call" | custom-call | tf_op jit(solution)/shard_map/hand_out/pallas_call | solution.py:550
